TPU v7x, 512 devices: a whole 4x4x16 slice. The times are simulated.
512 devices in a mesh: gx: 4 (over y), gy: 4 (over x), gz: 32 (over z, core).
Axes of the slice: x: 4, y: 4, z: 16, core: 2. Of those that a mesh axis runs over, the one named last changes fastest.
Arguments:
- seg_offset: float32 [3, 16, 4, 32, 256], P(None, 'gx', 'gy', 'gz'), may hold values from 0 to 1
- seg_vector: float32 [3, 16, 4, 32, 256], P(None, 'gx', 'gy', 'gz'), may hold values from -1.8 to 1.8
- burgers: float32 [3, 16, 4, 32, 256], P(None, 'gx', 'gy', 'gz'), may hold values from -6 to 6
- cell_counts: int32 [16, 4, 32], P('gx', 'gy', 'gz'), may hold values from 1 to 256, as said below
- applied: float32 [3, 3], replicated, may hold values from -4 to 4
Outputs:
- forces: float32 [3, 16, 4, 32, 256], P(None, 'gx', 'gy', 'gz')
Inputs may be any that keep to these rules, and one draw needn't show every extreme that they name: `cell_counts`: A cell's live segments fill its first slots; some cell is full.
All inputs are finite; a program needn't handle non-finite values.
Results may differ from a plain program's by a relative error of at most 0.0003.
Values sent between devices are 32-bit elements; how exact they have to be, the bound alone decides.
No kernel may reach another device: no remote copies, remote signals or barrier semaphores. Data moves between devices by JAX's collectives and lax.ppermute only.
A program may use at most 64 MiB of HBM per device.

v0:
```python
import math

import jax
import jax.numpy as jnp
import numpy as np
from jax import lax
from jax.sharding import PartitionSpec as P

CORE_WIDTH = 0.2
FIRST_COEF = 1.0 / (8.0 * math.pi)
SECOND_COEF = 1.0 / (4.0 * math.pi * 0.7)
NEIGHBOURS = np.array(
    [
        [step_x, step_y, step_z]
        for step_x in (-1, 0, 1)
        for step_y in (-1, 0, 1)
        for step_z in (-1, 0, 1)
    ],
    dtype=np.int32,
)


def extended(shard, sides, width):
    for axis, dim in sides:
        devices, length = (lax.axis_size(axis), shard.shape[dim])
        up = [(i, (i + 1) % devices) for i in range(devices - 1)]
        down = [(j, i) for i, j in up]
        last = lax.slice_in_dim(shard, length - width, length, axis=dim)
        initial = lax.slice_in_dim(shard, 0, width, axis=dim)
        before = lax.ppermute(last, axis, up)
        after = lax.ppermute(initial, axis, down)
        shard = jnp.concatenate([before, shard, after], axis=dim)
    return shard


def dotted(left_vec, right_vec):
    return left_vec[0] * right_vec[0] + left_vec[1] * right_vec[1] + left_vec[2] * right_vec[2]


def crossed(left_vec, right_vec):
    return (
        left_vec[1] * right_vec[2] - left_vec[2] * right_vec[1],
        left_vec[2] * right_vec[0] - left_vec[0] * right_vec[2],
        left_vec[0] * right_vec[1] - left_vec[1] * right_vec[0],
    )


def factors(apart):
    square = dotted(apart, apart) + CORE_WIDTH * CORE_WIDTH
    inverse = lax.rsqrt(square)
    recip_cube = inverse * inverse * inverse
    recip_fifth = recip_cube * inverse * inverse
    radial = 2.0 * recip_cube + 3.0 * CORE_WIDTH * CORE_WIDTH * recip_fifth
    return (recip_cube, recip_fifth, radial)


def pair_sum(apart, tangent, burgers_src, wedges, target, axis_sum):
    recip_cube, recip_fifth, radial = factors(apart)
    turned = crossed(apart, burgers_src)
    tangent_dot = dotted(tangent, target)
    turned_dot = dotted(turned, target)
    wedge_dot = dotted(wedges, target)
    apart_dot = dotted(apart, target)
    wedge_apart = dotted(wedges, apart)
    first_part = wedge_apart * (radial - recip_cube)
    third_part = 3.0 * wedge_apart * apart_dot * recip_fifth
    pieces = []
    for which in range(3):
        summand = -FIRST_COEF * radial * (
            turned[which] * tangent_dot + tangent[which] * turned_dot
        ) + SECOND_COEF * (
            target[which] * first_part
            - (wedges[which] * apart_dot + apart[which] * wedge_dot) * recip_cube
            + apart[which] * third_part
        )
        pieces.append(jnp.sum(summand, axis=axis_sum))
    return jnp.stack(pieces)


def distant_sum(apart, moment, distant):
    recip_cube, recip_fifth, radial = factors(apart)
    wedges = (moment[5] - moment[7], moment[6] - moment[2], moment[1] - moment[3])
    wedge_apart = dotted(wedges, apart)
    turned = [
        crossed(apart, (moment[column], moment[3 + column], moment[6 + column]))
        for column in range(3)
    ]
    pieces = []
    for row_axis in range(3):
        for col_axis in range(3):
            element = -FIRST_COEF * radial * (
                turned[col_axis][row_axis] + turned[row_axis][col_axis]
            ) + SECOND_COEF * (
                3.0 * wedge_apart * apart[row_axis] * apart[col_axis] * recip_fifth
                - (wedges[row_axis] * apart[col_axis] + wedges[col_axis] * apart[row_axis])
                * recip_cube
            )
            if row_axis == col_axis:
                element = element + SECOND_COEF * wedge_apart * (radial - recip_cube)
            pieces.append(jnp.sum(jnp.where(distant, element, 0.0), axis=-1))
    return jnp.stack(pieces)


def local_coords(cells_y, cells_z, flat):
    return (flat // (cells_y * cells_z), flat // cells_z % cells_y, flat % cells_z)


def full_shell(ghost_src, own_src, cells_x, cells_y, cells_z):
    per_device = cells_x * cells_y * cells_z
    width = own_src.shape[-1]
    anchor = jnp.zeros((), jnp.int32)

    def visit_all(running, offset_row):
        corner = offset_row + 1
        source_block = lax.dynamic_slice(
            ghost_src,
            (anchor, corner[0], corner[1], corner[2], anchor),
            (12, cells_x, cells_y, cells_z, width),
        ).reshape(12, per_device, width)
        apart = (
            own_src[0:3, :, :, None]
            - source_block[0:3, :, None, :]
            - offset_row.astype(jnp.float32)[:, None, None, None]
        )
        return (
            running
            + pair_sum(
                apart,
                source_block[3:6, :, None, :],
                source_block[6:9, :, None, :],
                source_block[9:12, :, None, :],
                own_src[6:9, :, :, None],
                -1,
            ),
            None,
        )

    result, unused = lax.scan(
        visit_all, jnp.zeros((3, per_device, width), jnp.float32), jnp.asarray(NEIGHBOURS)
    )
    return result


def local(seg_offset, seg_vector, burgers, cell_counts, applied):
    leading, cells_x, cells_y, cells_z, slot_count = seg_offset.shape
    per_device = cells_x * cells_y * cells_z
    slot_ids = jnp.arange(slot_count, dtype=jnp.int32)
    filled = slot_ids[None, None, None, :] < cell_counts[..., None]
    tangent_live = jnp.where(filled[None], seg_vector, 0.0)
    burgers_live = jnp.where(filled[None], burgers, 0.0)
    wedges = jnp.stack(crossed(burgers_live, tangent_live))
    outgoing = jnp.concatenate([seg_offset, tangent_live, burgers_live])
    ghosted = extended(outgoing, (("gx", 1), ("gy", 2), ("gz", 3)), 1)
    ghosted = jnp.concatenate([ghosted, jnp.stack(crossed(ghosted[6:9], ghosted[3:6]))])
    owned = jnp.concatenate([outgoing, wedges]).reshape(12, per_device, slot_count)
    nearby = full_shell(ghosted, owned, cells_x, cells_y, cells_z)
    span_y = lax.axis_size("gy")
    span_z = lax.axis_size("gz")
    flat = jnp.arange(per_device, dtype=jnp.int32)
    place_x, place_y, place_z = local_coords(cells_y, cells_z, flat)
    owned_coords = jnp.stack(
        [
            lax.axis_index("gx") * cells_x + place_x,
            lax.axis_index("gy") * cells_y + place_y,
            lax.axis_index("gz") * cells_z + place_z,
        ]
    ).astype(jnp.float32)
    moment = jnp.sum(burgers_live[:, None] * tangent_live[None, :], axis=-1).reshape(9, per_device)
    shard_piece = lax.all_gather(moment, ("gx", "gy", "gz"), axis=1, tiled=True)
    columns = jnp.arange(shard_piece.shape[1], dtype=jnp.int32)
    device_id = columns // per_device
    within_x, within_y, within_z = local_coords(cells_y, cells_z, columns % per_device)
    sources = jnp.stack(
        [
            device_id // (span_y * span_z) * cells_x + within_x,
            device_id // span_z % span_y * cells_y + within_y,
            device_id % span_z * cells_z + within_z,
        ]
    ).astype(jnp.float32)
    apart = owned_coords[:, :, None] - sources[:, None, :]
    distant = jnp.max(jnp.abs(apart), axis=0) > 1.5
    distant_stress = distant_sum(apart, shard_piece[:, None, :], distant)
    symmetric = 0.5 * (applied + applied.T)
    stress = distant_stress + symmetric.reshape(9)[:, None]
    burgers_flat = burgers_live.reshape(3, per_device, slot_count)
    rows = []
    for row_axis in range(3):
        rows.append(
            stress[row_axis * 3][:, None] * burgers_flat[0]
            + stress[row_axis * 3 + 1][:, None] * burgers_flat[1]
            + stress[row_axis * 3 + 2][:, None] * burgers_flat[2]
        )
    total = nearby + jnp.stack(rows)
    forces = jnp.stack(crossed(total, tangent_live.reshape(3, per_device, slot_count)))
    return forces.reshape(3, cells_x, cells_y, cells_z, slot_count)


def solution(mesh):
    placed = (
        P(None, "gx", "gy", "gz", None),
        P(None, "gx", "gy", "gz", None),
        P(None, "gx", "gy", "gz", None),
        P("gx", "gy", "gz"),
        P(),
    )
    return jax.shard_map(
        local,
        mesh=mesh,
        in_specs=placed,
        out_specs=P(None, "gx", "gy", "gz", None),
        check_vma=False,
    )
```

profile of v0, /device:TPU:1, one launch (start us, length us, event | category | flops | bytes accessed | tf_op | source)
XLA Modules:
  0.0 498.2 jit_solution(2668501754419563898)
XLA Ops:
  2.9 4.0 collective-permute-start
  7.0 1.3 collective-permute-start.1
  8.5 142.0 %all-gather = f32[512,4,9]{2,1,0:T(4,128)S(1)} all-gather(f32[1,4,9]{2,1,0:T(4,128)S(1)} %bitcast.287), channel_id=1, replica_groups=mesh['gx'=4,'gy'=4,'gz'=32] {'gx','gy','gz'}, dimensions={0}, use_global_device_ids=true | all-gather | bytes 73872 | tf_op jit(solution)/shard_map/all_gather | solution.py:169
  153.6 2.6 collective-permute-start.2
  156.3 1.3 collective-permute-start.3
  157.7 3.7 collective-permute-done.3
  161.4 3.4 collective-permute-start.4
  164.8 1.9 collective-permute-start.5
  166.7 0.9 collective-permute-done.4
  167.7 4.4 collective-permute-done.5
  172.3 325.2 %while.12 = (s32[]{:T(128)}, f32[3,4,256]{2,1,0:T(4,128)S(1)}, f32[12,4,256]{2,1,0:T(4,128)S(1)}, f32[12,6,3,3,256]{4,1,3,2,0:T(8,128)S(1)}, s32[]{:T(128)}, /*i...) while((s32[]{:T(128)}, f32[3,4,256]{2,1,0:T(4,128)S(1)}, ...), condition=%wide.region_4.5_spmd.clone.clone, body=%wide.region_0.4_spmd.sunk.clone.clone.sunk | while | flops 27272216 | bytes 20206088 | solution.py:138
  179.9 0.8 multiply_subtract_fusion.7
  180.7 3.6 add_reduce_fusion.4
  191.9 0.8 multiply_subtract_fusion.7
  192.7 3.6 add_reduce_fusion.4
  204.0 0.8 multiply_subtract_fusion.7
  204.8 3.6 add_reduce_fusion.4
  216.0 0.8 multiply_subtract_fusion.7
  216.8 3.6 add_reduce_fusion.4
  228.1 0.8 multiply_subtract_fusion.7
  228.9 3.6 add_reduce_fusion.4
  240.9 3.6 add_reduce_fusion.4
  252.2 0.8 multiply_subtract_fusion.7
  253.0 3.6 add_reduce_fusion.4
  265.0 3.6 add_reduce_fusion.4
  276.3 0.8 multiply_subtract_fusion.7
  277.1 3.6 add_reduce_fusion.4
  289.1 3.6 add_reduce_fusion.4
  300.4 0.8 multiply_subtract_fusion.7
  301.2 3.6 add_reduce_fusion.4
  313.2 3.6 add_reduce_fusion.4
  324.5 0.8 multiply_subtract_fusion.7
  325.2 3.6 add_reduce_fusion.4
  337.3 3.6 add_reduce_fusion.4
  349.3 3.6 add_reduce_fusion.4
  361.4 3.6 add_reduce_fusion.4
  373.4 3.6 add_reduce_fusion.4
  385.5 3.6 add_reduce_fusion.4
  397.5 3.6 add_reduce_fusion.4
  409.6 3.6 add_reduce_fusion.4
  421.6 3.6 add_reduce_fusion.4
  433.7 3.6 add_reduce_fusion.4
  445.7 3.6 add_reduce_fusion.4
  457.7 3.6 add_reduce_fusion.4
  469.8 3.6 add_reduce_fusion.4
  481.0 0.8 multiply_subtract_fusion.7
  481.8 3.6 add_reduce_fusion.4
  493.9 3.6 add_reduce_fusion.4
  (287 shorter events, 72.4 us)
Async XLA Ops:
  0.0 152.9 %copy-start = (f32[3,3]{1,0:T(4,128)S(1)}, f32[3,3]{1,0:T(4,128)}, u32[]{:S(2)}) copy-start(f32[3,3]{1,0:T(4,128)} %param.12) | copy-start | bytes 112
  2.9 150.7 %collective-permute-start = (f32[9,1,1,1,256]{4,1,3,2,0:T(1,128)S(1)}, f32[9,1,1,1,256]{4,1,3,2,0:T(1,128)S(1)}, u32[]{:S(2)}, u32[]{:S(2)}) collective-permute-start(f32[9,1,1,1,256]{4,1,3,2,0:T(1,128)S(1)} %get-tuple-element.154), channel_id=1, source_target_pairs={{0,128},{128,256},{256,384},{1,129},{129,257},{257,385},{2,130},{1... | collective-permute-start | bytes 27656 | tf_op jit(solution)/shard_map/ppermute | solution.py:30
  7.0 146.7 %collective-permute-start.1 = (f32[9,1,1,1,256]{4,1,3,2,0:T(1,128)S(1)}, f32[9,1,1,1,256]{4,1,3,2,0:T(1,128)S(1)}, u32[]{:S(2)}, u32[]{:S(2)}) collective-permute-start(f32[9,1,1,1,256]{4,1,3,2,0:T(1,128)S(1)} %get-tuple-element.155), channel_id=1, source_target_pairs={{128,0},{256,128},{384,256},{129,1},{257,129},{385,257},{130,2},{2... | collective-permute-start | bytes 27656 | tf_op jit(solution)/shard_map/ppermute | solution.py:31
  153.6 4.0 collective-permute-start.2
  156.3 5.1 %collective-permute-start.3 = (f32[9,6,1,1,256]{4,1,3,2,0:T(8,128)S(1)}, f32[9,6,1,1,256]{4,1,3,2,0:T(8,128)S(1)}, u32[]{:S(2)}, u32[]{:S(2)}) collective-permute-start(f32[9,6,1,1,256]{4,1,3,2,0:T(8,128)S(1)} %pad_maximum_fusion.3), channel_id=1, source_target_pairs={{32,0},{64,32},{96,64},{33,1},{65,33},{97,65},{34,2},{66,34},{98,6... | collective-permute-start | bytes 165896 | tf_op jit(solution)/shard_map/ppermute | solution.py:31
  161.4 6.2 %collective-permute-start.4 = (f32[9,6,3,1,256]{4,1,3,2,0:T(8,128)S(1)}, f32[9,6,3,1,256]{4,1,3,2,0:T(8,128)S(1)}, u32[]{:S(2)}, u32[]{:S(2)}) collective-permute-start(f32[9,6,3,1,256]{4,1,3,2,0:T(8,128)S(1)} %pad_maximum_fusion.2), channel_id=1, source_target_pairs={{0,1},{1,2},{2,3},{3,4},{4,5},{5,6},{6,7},{7,8},{8,9},{9,10},{10,1... | collective-permute-start | bytes 497672 | tf_op jit(solution)/shard_map/ppermute | solution.py:30
  164.8 7.3 %collective-permute-start.5 = (f32[9,6,3,1,256]{4,1,3,2,0:T(8,128)S(1)}, f32[9,6,3,1,256]{4,1,3,2,0:T(8,128)S(1)}, u32[]{:S(2)}, u32[]{:S(2)}) collective-permute-start(f32[9,6,3,1,256]{4,1,3,2,0:T(8,128)S(1)} %pad_maximum_fusion.2), channel_id=1, source_target_pairs={{1,0},{2,1},{3,2},{4,3},{5,4},{6,5},{7,6},{8,7},{9,8},{10,9},{11,1... | collective-permute-start | bytes 497672 | tf_op jit(solution)/shard_map/ppermute | solution.py:31
where the time goes:
time: 502 us; the launch traced here: 498 us
  loops' own time  155 us (31%)
  other arithmetic  154 us (31%)
  blocking collectives  142 us (28%)
  local copies, waits for them, and re-layouts  23.2 us (5%)
  starting transfers between devices  14.5 us (3%)
  waiting for transfers between devices  9.09 us (2%)
    another operation x1, loops' own time, full_shell(): lax.scan(visit_all, jnp.zeros((3, per_device, width), jnp.float32), jnp.a...  155 us
    all_gather x1, blocking collectives, local(): shard_piece = lax.all_gather(moment, ('gx', 'gy', 'gz'), axis=1, tiled=True)  142 us
    reduce_sum x27, other arithmetic, pair_sum(): pieces.append(jnp.sum(summand, axis=axis_sum))  97.7 us
    sub x27, other arithmetic, crossed(): left_vec[2] * right_vec[0] - left_vec[0] * right_vec[2]  20.9 us
    add x27, other arithmetic, visit_all(): corner = offset_row + 1  18.9 us
    slice x27, local copies, waits for them, and re-layouts, visit_all(): corner[2]  18.1 us
    sub x27, other arithmetic, visit_all(): own_src[0:3, :, :, None] - source_block[0:3, :, None, :]  12.8 us
  transfers between devices with their start and end apart: 6, of which 4 were waited for; matrix products, arithmetic and copies ran while one was open for 1% of the time, Pallas kernels for 0%

commit v1 on v0

v1 whole, which is shorter than its diff:
```python
import functools
import math

import jax
import jax.numpy as jnp
from jax import lax
from jax.experimental import pallas as pl
from jax.experimental.pallas import tpu as pltpu
from jax.sharding import PartitionSpec as P

CORE_SQUARE = 0.2 * 0.2
FIRST = 1.0 / (8.0 * math.pi)
SECOND = 1.0 / (4.0 * math.pi * 0.7)
KAPPA = 3.0 * CORE_SQUARE
CAP = 256
LANES = 128
ROWS = 10
PAIRS = ((0, 0), (0, 1), (0, 2), (1, 1), (1, 2), (2, 2))
NUM3 = 32
NUM5 = 48


def cross(a, b):
    return (
        a[1] * b[2] - a[2] * b[1],
        a[2] * b[0] - a[0] * b[2],
        a[0] * b[1] - a[1] * b[0],
    )


def plus(terms):
    terms = [t for t in terms if t is not None]
    total = terms[0]
    for t in terms[1:]:
        total = total + t
    return total


def features(y, t, b):
    w = cross(b, t)
    turn = [[None, b[2], -b[1]], [-b[2], None, b[0]], [b[1], -b[0], None]]
    c2w = [SECOND * v for v in w]
    lin3, lin5 = {}, {}
    for n, (i, j) in enumerate(PAIRS):
        for m in range(3):
            parts = []
            if turn[i][m] is not None:
                parts.append(turn[i][m] * t[j])
            if turn[j][m] is not None:
                parts.append(turn[j][m] * t[i])
            base = plus(parts) * (-FIRST) if parts else None
            a3 = [2.0 * base] if base is not None else []
            a5 = [base] if base is not None else []
            if i == j:
                a3.append(c2w[m])
                a5.append(c2w[m])
            if m == j:
                a3.append(-c2w[i])
            if m == i:
                a3.append(-c2w[j])
            lin3[m, n] = plus(a3) if a3 else None
            lin5[m, n] = KAPPA * plus(a5) if a5 else None
    w3 = [3.0 * v for v in c2w]
    wy = [[w3[m] * y[n] for n in range(3)] for m in range(3)]
    dot = wy[0][0] + wy[1][1] + wy[2][2]
    doty = [dot * y[n] for n in range(3)]
    rows3, rows5 = {}, {}
    for n, (i, j) in enumerate(PAIRS):
        zero3, zero5 = [], [doty[i] * y[j]]
        for m in range(3):
            if lin3[m, n] is not None:
                rows3[8 * m + n] = lin3[m, n]
                zero3.append(lin3[m, n] * y[m])
            quad = [wy[m][i] * y[j]]
            if m == i:
                quad.append(doty[j])
            if m == j:
                quad.append(doty[i])
            if lin5[m, n] is not None:
                quad.append(lin5[m, n])
                zero5.append(lin5[m, n] * y[m])
            rows5[8 * m + n] = plus(quad)
        if zero3:
            rows3[24 + n] = -plus(zero3)
        rows5[24 + n] = -plus(zero5)
    for m in range(3):
        for n in range(3):
            rows5[32 + 3 * m + n] = -wy[m][n]
        rows5[41 + m] = w3[m]
    return rows3, rows5


def halves(value, terms):
    out = []
    for k in range(terms):
        part = value.astype(jnp.bfloat16)
        out.append(part)
        if k + 1 < terms:
            value = value - part.astype(jnp.float32)
    return out


def near_kernel(planes, offsets, counts_ref, *refs):
    sources = refs[: len(offsets)]
    refs = refs[len(offsets):]
    own_ref, out_ref = refs[:2]
    raw, feat, wide, left3, left5, live_ref = refs[2:]
    columns = [(k, c, d) for k, group in enumerate(offsets) for c, d in enumerate(group)]
    blocks = -(-(2 * len(columns) + 1) // 8) * 8
    chunks = blocks // 2
    lane = lax.broadcasted_iota(jnp.int32, (ROWS, LANES), 1)
    lift = lax.broadcasted_iota(jnp.int32, (ROWS, LANES), 0)

    raw[...] = jnp.zeros_like(raw)
    feat[...] = jnp.zeros_like(feat)
    out_ref[...] = jnp.zeros_like(out_ref)

    for j in range(planes):
        at = jnp.int32(0)
        for k, c, (dy, dz) in columns:
            cell = c * planes + j
            shift = (
                jnp.where(lift < 3, -0.5, 0.0)
                + jnp.where(lift == 1, float(dy), 0.0)
                + jnp.where(lift == 2, float(dz), 0.0)
            )
            first = sources[k][ROWS * cell: ROWS * cell + ROWS, 0:LANES] + shift
            second = sources[k][ROWS * cell: ROWS * cell + ROWS, LANES:] + shift
            low = jnp.bitwise_and(at, LANES - 1)
            base = lax.shift_right_logical(at, 7) + j * blocks
            first = pltpu.roll(first, low, 1)
            second = pltpu.roll(second, low, 1)
            keep = lane >= low
            place = pl.multiple_of(base * 16, 16)
            raw[pl.ds(place, ROWS), :] = jnp.where(keep, first, raw[pl.ds(place, ROWS), :])
            raw[pl.ds(place + 16, ROWS), :] = jnp.where(keep, second, first)
            raw[pl.ds(place + 32, ROWS), :] = jnp.where(keep, 0.0, second)
            at = at + counts_ref[k * len(offsets[k]) * planes + cell]
        live_ref[j] = at

    def plane_body(j, carry):
        live = live_ref[j]
        groups = lax.shift_right_logical(live + 8 * LANES - 1, 10)
        steps = lax.shift_right_logical(live + CAP - 1, 8)

        def group_body(g, carry):
            start = pl.multiple_of((j * blocks + g * 8) * 16, 128)
            row = [raw[pl.ds(start + r, 8, stride=16), :] for r in range(9)]
            rows3, rows5 = features(row[0:3], row[3:6], row[6:9])
            for r, value in rows3.items():
                feat[pl.ds(r, 8, stride=NUM3 + NUM5), :] = value
            for r, value in rows5.items():
                feat[pl.ds(NUM3 + r, 8, stride=NUM3 + NUM5), :] = value
            for q in range(8):
                piece = halves(feat[q * 80: q * 80 + NUM3, :], 3)
                span = slice((q % 2) * LANES, (q % 2 + 1) * LANES)
                for n in range(3):
                    left3[g * 4 + q // 2, n * NUM3: (n + 1) * NUM3, span] = piece[n]
                piece = halves(feat[q * 80 + NUM3: (q + 1) * 80, :], 3)
                for n in range(3):
                    left5[g * 4 + q // 2, n * NUM5: (n + 1) * NUM5, span] = piece[n]
                turned = jnp.transpose(raw[pl.ds(start + q * 16, 8), :])
                for n in range(3):
                    wide[g * 4 + q // 2, n, (q % 2) * LANES: (q % 2 + 1) * LANES, :] = (
                        jnp.broadcast_to(turned[:, n: n + 1], (LANES, LANES))
                    )
            return carry

        lax.fori_loop(0, groups, group_body, 0)

        def cell_body(i, carry):
            where_x = (i + 1 - j).astype(jnp.float32) - 0.5
            points = [
                own_ref[i, 0:1, :] + where_x,
                own_ref[i, 1:2, :] - 0.5,
                own_ref[i, 2:3, :] - 0.5,
            ]
            targets = counts_ref[counts_ref.shape[0] - 4 + i]

            def run(parts):
                width = parts * LANES
                seen = [
                    [jnp.broadcast_to(v[:, h * LANES:(h + 1) * LANES], (16, LANES)) for v in points]
                    for h in range(parts)
                ]

                def step(c, acc):
                    acc3, acc5 = acc
                    high3, low3, high5, low5 = [], [], [], []
                    for s in range(CAP // 16):
                        there = [wide[c, n, s * 16: (s + 1) * 16, :] for n in range(3)]
                        got = [[], [], [], []]
                        for h in range(parts):
                            d = [seen[h][n] - there[n] for n in range(3)]
                            inv = lax.rsqrt(d[0] * d[0] + d[1] * d[1] + (d[2] * d[2] + CORE_SQUARE))
                            square = inv * inv
                            cube = square * inv
                            fifth = cube * square
                            a, b = halves(cube, 2)
                            e, f = halves(fifth, 2)
                            for store, value in zip(got, (a, b, e, f)):
                                store.append(value)
                        for store, value in zip((high3, low3, high5, low5), got):
                            store.append(jnp.concatenate(value, axis=1) if parts > 1 else value[0])
                    high3, low3, high5, low5 = [
                        jnp.concatenate(v, axis=0) for v in (high3, low3, high5, low5)
                    ]
                    mm = functools.partial(jnp.dot, preferred_element_type=jnp.float32)
                    a = mm(left3[c], high3)
                    b = mm(left3[c, 0:2 * NUM3, :], low3)
                    acc3 = acc3 + (
                        a[0:NUM3]
                        + (a[NUM3:2 * NUM3] + b[0:NUM3])
                        + (a[2 * NUM3:] + b[NUM3:])
                    )
                    a = mm(left5[c], high5)
                    b = mm(left5[c, 0:2 * NUM5, :], low5)
                    acc5 = acc5 + (
                        a[0:NUM5]
                        + (a[NUM5:2 * NUM5] + b[0:NUM5])
                        + (a[2 * NUM5:] + b[NUM5:])
                    )
                    return acc3, acc5

                acc3, acc5 = lax.fori_loop(
                    0,
                    steps,
                    step,
                    (jnp.zeros((NUM3, width), jnp.float32), jnp.zeros((NUM5, width), jnp.float32)),
                )
                x = [v[:, 0:width] for v in points]
                both = acc3 + acc5[0:NUM3]
                linear = both[24:32] + x[0] * both[0:8] + x[1] * both[8:16] + x[2] * both[16:24]
                second = acc5[32:48]
                v = [
                    x[0] * second[n: n + 1] + x[1] * second[3 + n: 4 + n] + x[2] * second[6 + n: 7 + n]
                    for n in range(3)
                ]
                scale = 0.5 * (
                    second[0:1] + second[4:5] + second[8:9]
                    + x[0] * second[9:10] + x[1] * second[10:11] + x[2] * second[11:12]
                )
                v = [v[n] + scale * x[n] for n in range(3)]
                for n, (a, b) in enumerate(PAIRS):
                    out_ref[i, n: n + 1, 0:width] += linear[n: n + 1] + x[a] * v[b] + x[b] * v[a]

            @pl.when(targets > LANES)
            def _():
                run(2)

            @pl.when(targets <= LANES)
            def _():
                run(1)

            return carry

        lax.fori_loop(jnp.maximum(j - 2, 0), jnp.minimum(j + 1, planes - 2), cell_body, 0)
        return carry

    lax.fori_loop(0, planes, plane_body, 0)


def near(planes, offsets, counts, sources, own):
    columns = sum(len(group) for group in offsets)
    blocks = -(-(2 * columns + 1) // 8) * 8
    cells = planes - 2
    vmem = pl.BlockSpec(memory_space=pltpu.VMEM)
    return pl.pallas_call(
        functools.partial(near_kernel, planes, offsets),
        out_shape=jax.ShapeDtypeStruct((cells, 8, CAP), jnp.float32),
        in_specs=[pl.BlockSpec(memory_space=pltpu.SMEM)] + [vmem] * (len(sources) + 1),
        out_specs=vmem,
        scratch_shapes=[
            pltpu.VMEM((planes * blocks * 16, LANES), jnp.float32),
            pltpu.VMEM((8 * (NUM3 + NUM5), LANES), jnp.float32),
            pltpu.VMEM((blocks // 2, 3, CAP, LANES), jnp.float32),
            pltpu.VMEM((blocks // 2, 3 * NUM3, CAP), jnp.bfloat16),
            pltpu.VMEM((blocks // 2, 3 * NUM5, CAP), jnp.bfloat16),
            pltpu.SMEM((planes,), jnp.int32),
        ],
        compiler_params=pltpu.CompilerParams(vmem_limit_bytes=32 * 1024 * 1024),
        name="near_%d" % columns,
    )(counts, *sources, own)


def far_kernel(spans, moment_ref, place_ref, applied_ref, own_ref, *refs):
    parts, out_ref = refs[:-1], refs[-1]
    span_y, span_z = spans
    cells = own_ref.shape[0]
    count = moment_ref.shape[0]
    turned = jnp.transpose(moment_ref[...])
    moment = [turned[cells * m: cells * m + cells, :] for m in range(9)]
    device = lax.broadcasted_iota(jnp.int32, (cells, count), 1)
    inner = lax.broadcasted_iota(jnp.int32, (cells, count), 0)
    source = (
        (device // (span_y * span_z) * cells + inner).astype(jnp.float32),
        (device // span_z % span_y).astype(jnp.float32),
        (device % span_z).astype(jnp.float32),
    )
    w = (moment[5] - moment[7], moment[6] - moment[2], moment[1] - moment[3])
    index = {}
    for n, (a, b) in enumerate(PAIRS):
        index[a, b] = index[b, a] = n
    for i in range(cells):
        mine = (place_ref[0] * cells + i, place_ref[1], place_ref[2])
        r = [mine[n].astype(jnp.float32) - source[n] for n in range(3)]
        reach = jnp.maximum(jnp.maximum(jnp.abs(r[0]), jnp.abs(r[1])), jnp.abs(r[2]))
        inv = lax.rsqrt(r[0] * r[0] + r[1] * r[1] + r[2] * r[2] + CORE_SQUARE)
        inv = jnp.where(reach > 1.5, inv, 0.0)
        cube = inv * inv * inv
        fifth = cube * inv * inv
        radial = 2.0 * cube + KAPPA * fifth
        along = w[0] * r[0] + w[1] * r[1] + w[2] * r[2]
        turn = [cross(r, (moment[n], moment[3 + n], moment[6 + n])) for n in range(3)]
        slope = (3.0 * SECOND) * along * fifth
        cut = SECOND * cube
        bulk = SECOND * along * (radial - cube)
        front = -FIRST * radial
        stress = []
        for n, (a, b) in enumerate(PAIRS):
            element = (
                front * (turn[b][a] + turn[a][b])
                + slope * r[a] * r[b]
                - cut * (w[a] * r[b] + w[b] * r[a])
            )
            if a == b:
                element = element + bulk
            stress.append(
                jnp.sum(element, axis=(0, 1), keepdims=True)
                + 0.5 * (applied_ref[a, b] + applied_ref[b, a])
                + plus([part[i, n: n + 1, :] for part in parts])
            )
        t = [own_ref[i, 3 + n: 4 + n, :] for n in range(3)]
        b = [own_ref[i, 6 + n: 7 + n, :] for n in range(3)]
        force = [plus([stress[index[m, n]] * b[n] for n in range(3)]) for m in range(3)]
        for n, value in enumerate(cross(force, t)):
            out_ref[n, i: i + 1, :] = value


def far(spans, moments, place, applied, own, parts):
    cells = own.shape[0]
    vmem = pl.BlockSpec(memory_space=pltpu.VMEM)
    smem = pl.BlockSpec(memory_space=pltpu.SMEM)
    return pl.pallas_call(
        functools.partial(far_kernel, spans),
        out_shape=jax.ShapeDtypeStruct((3, cells, CAP), jnp.float32),
        in_specs=[vmem, smem, smem, vmem] + [vmem] * len(parts),
        out_specs=vmem,
        compiler_params=pltpu.CompilerParams(vmem_limit_bytes=32 * 1024 * 1024),
        name="far",
    )(moments, place, applied, own, *parts)


def beside(first, last, axis):
    devices = lax.axis_size(axis)
    up = [(i, i + 1) for i in range(devices - 1)]
    down = [(i + 1, i) for i in range(devices - 1)]
    return lax.ppermute(last, axis, up), lax.ppermute(first, axis, down)


def local(seg_offset, seg_vector, burgers, cell_counts, applied):
    cells = seg_offset.shape[1]
    planes = cells + 2
    counts = cell_counts.reshape(cells)
    slots = jnp.arange(CAP, dtype=jnp.int32)
    filled = slots[None, :] < counts[:, None]
    offset = seg_offset.reshape(3, cells, CAP)
    tangent = jnp.where(filled[None], seg_vector.reshape(3, cells, CAP), 0.0)
    charge = jnp.where(filled[None], burgers.reshape(3, cells, CAP), 0.0)
    moment = jnp.sum(charge[:, None] * tangent[None, :], axis=-1).reshape(1, 9 * cells)
    moments = gathered(jnp.pad(moment, ((0, 0), (0, LANES - 9 * cells))))
    level = jnp.broadcast_to(counts.astype(jnp.float32)[None, :, None], (1, cells, CAP))
    own = jnp.concatenate([offset, tangent, charge, level]).transpose(1, 0, 2)
    flat = own.reshape(cells * ROWS, CAP)
    before, after = beside(flat[:ROWS], flat[-ROWS:], "gx")
    column = jnp.concatenate([before, flat, after])
    before, after = beside(column, column, "gy")
    sheet = jnp.concatenate([before, column, after])
    before, after = beside(sheet, sheet, "gz")

    def live(array):
        return array.reshape(-1, ROWS, CAP)[:, ROWS - 1, 0].astype(jnp.int32)

    middle = [(dy, 0) for dy in (-1, 0, 1)]
    outer = [[(dy, dz) for dy in (-1, 0, 1)] for dz in (-1, 1)]
    near_a = near(planes, [middle], jnp.concatenate([live(sheet), counts]), [sheet], own)
    near_b = near(
        planes,
        outer,
        jnp.concatenate([live(before), live(after), counts]),
        [before, after],
        own,
    )
    place = jnp.stack([lax.axis_index(a) for a in ("gx", "gy", "gz")]).astype(jnp.int32)
    spans = (lax.axis_size("gy"), lax.axis_size("gz"))
    result = far(spans, moments, place, applied, own, [near_a, near_b])
    return result.reshape(seg_offset.shape)


def gathered(moment):
    wide = jnp.concatenate([moment] * 8, axis=0)
    whole = lax.all_gather(wide, ("gx", "gy", "gz"), axis=0, tiled=True)
    return whole.reshape(-1, 8, LANES)[:, 0, :]


def solution(mesh):
    placed = P(None, "gx", "gy", "gz", None)
    return jax.shard_map(
        local,
        mesh=mesh,
        in_specs=(placed, placed, placed, P("gx", "gy", "gz"), P()),
        out_specs=placed,
        check_vma=False,
    )
```

time: 502 us -> 222 us (0.44)
  loops' own time: 155 us -> 0 us
  other arithmetic: 154 us -> 4.47 us
  waiting for transfers between devices: 9.09 us -> 155 us
  blocking collectives: 142 us -> 0 us
  Pallas kernels: 0 us -> 23.5 us
  local copies, waits for them, and re-layouts: 23.2 us -> 4.29 us
  between operations: 0.21 us -> 13.6 us
  starting transfers between devices: 14.5 us -> 20.9 us
    another operation x1 -> x0, loops' own time: 155 us -> none  [full_shell(): lax.scan(visit_all, jnp.zeros((3, per_device, width), jnp.float32), jnp.a...]
    all_gather x0 -> x1, waiting for transfers between devices: none -> 150 us  [gathered(): whole = lax.all_gather(wide, ('gx', 'gy', 'gz'), axis=0, tiled=True)]
    all_gather x1 -> x0, blocking collectives: 142 us -> none  [local(): shard_piece = lax.all_gather(moment, ('gx', 'gy', 'gz'), axis=1, tiled=True)]
    reduce_sum x30 -> x1, other arithmetic: 98.5 us -> 0.1 us  [local(): jnp.sum(charge[:, None] * tangent[None, :], axis=-1).reshape(1, 9 * cells)]
    sub x56 -> x0, other arithmetic: 33.8 us -> none  [the longest x27 20.9 us: crossed(): left_vec[2] * right_vec[0] - left_vec[0] * right_vec[2]]
    pallas_call x0 -> x3, Pallas kernels: none -> 23.5 us  [the longest x2 22.5 us: near(): pl.pallas_call(functools.partial(near_kernel, planes, offsets), out_shape...]
    add x59 -> x0, other arithmetic: 19.4 us -> none  [the longest x27 18.9 us: visit_all(): corner = offset_row + 1]
    slice x55 -> x2, local copies, waits for them, and re-layouts: 18.5 us -> 1.73 us  [the longest x1 1.73 us: gathered(): return whole.reshape(-1, 8, LANES)[:, 0, :]]
  transfers between devices with their start and end apart: 6 -> 7, of which waited for: 4 -> 3; matrix products, arithmetic and copies ran while one was open for 1% -> 2% of each run, Pallas kernels for 0% -> 10%
where the time goes in v1:
time: 222 us
  waiting for transfers between devices  155 us (70%)
  Pallas kernels  23.5 us (11%)
  starting transfers between devices  20.9 us (9%)
  between operations  13.6 us (6%)
  other arithmetic  4.47 us (2%)
  local copies, waits for them, and re-layouts  4.29 us (2%)
    all_gather x1, waiting for transfers between devices, gathered(): whole = lax.all_gather(wide, ('gx', 'gy', 'gz'), axis=0, tiled=True)  150 us
    pallas_call x2, Pallas kernels, near(): pl.pallas_call(functools.partial(near_kernel, planes, offsets), out_shape...  22.5 us
    ppermute x6, starting transfers between devices, beside(): return (lax.ppermute(last, axis, up), lax.ppermute(first, axis, down))  20.9 us
    ppermute x6, waiting for transfers between devices, beside(): return (lax.ppermute(last, axis, up), lax.ppermute(first, axis, down))  4.45 us
  transfers between devices with their start and end apart: 7, of which 3 were waited for; matrix products, arithmetic and copies ran while one was open for 2% of the time, Pallas kernels for 10%

profile of v1, /device:TPU:1, one launch (start us, length us, event | category | flops | bytes accessed | tf_op | source)
XLA Modules:
  0.0 221.7 jit_solution(18012471394521411054)
XLA Ops:
  6.5 0.0 copy-start.1
  6.5 0.0 copy-start
  6.5 0.0 all-gather.2.cloned.1.call-start
  6.5 0.8 iota_compare_fusion
  7.3 0.7 bitcast_select_fusion.1
  8.1 0.1 multiply_reduce_fusion
  8.2 0.1 reshape.77
  8.3 0.6 concatenate.19
  8.9 0.0 all-gather.2.cloned.1.call-update
  8.9 0.7 copy.40
  9.6 0.7 bitcast_convert_fusion
  10.3 0.1 broadcast_in_dim.29
  10.4 1.3 collective-permute-start.1
  11.7 4.7 %collective-permute-start = (f32[10,256]{1,0:T(8,128)S(1)}, f32[10,256]{1,0:T(8,128)S(1)}, u32[]{:S(2)}, u32[]{:S(2)}) collective-permute-start(f32[10,256]{1,0:T(8,128)S(1)} %get-tuple-element.5), channel_id=1, source_target_pairs={{0,128},{128,256},{256,384},{1,129},{129,257},{257,385},{2,130},{1... | collective-permute-start | bytes 30728 | tf_op jit(solution)/shard_map/ppermute | solution.py:358
  16.4 0.0 collective-permute-done.1
  16.4 0.8 collective-permute-done
  17.2 3.3 %collective-permute-start.2 = (f32[60,256]{1,0:T(8,128)S(1)}, f32[60,256]{1,0:T(8,128)S(1)}, u32[]{:S(2)}, u32[]{:S(2)}) collective-permute-start(f32[60,256]{1,0:T(8,128)S(1)} %pad_maximum_fusion), channel_id=1, source_target_pairs={{0,32},{32,64},{64,96},{1,33},{33,65},{65,97},{2,34},{34,66},{66,9... | collective-permute-start | bytes 184328 | tf_op jit(solution)/shard_map/ppermute | solution.py:358
  20.5 1.3 collective-permute-start.3
  21.8 0.1 pad_add_fusion.place_ref
  21.9 0.0 collective-permute-done.2
  21.9 3.6 %collective-permute-done.3 = f32[60,256]{1,0:T(8,128)S(1)} collective-permute-done((f32[60,256]{1,0:T(8,128)S(1)}, f32[60,256]{1,0:T(8,128)S(1)}, u32[]{:S(2)}, u32[]{:S(2)}) %collective-permute-start.3) | collective-permute-done | bytes 61472 | tf_op jit(solution)/shard_map/ppermute | solution.py:358
  25.5 0.4 concatenate.22.refs_0_
  25.9 8.4 %collective-permute-start.5 = (f32[180,256]{1,0:T(8,128)S(1)}, f32[180,256]{1,0:T(8,128)S(1)}, u32[]{:S(2)}, u32[]{:S(2)}) collective-permute-start(f32[180,256]{1,0:T(8,128)S(1)} %concatenate.22.refs_0_), channel_id=1, source_target_pairs={{1,0},{2,1},{3,2},{4,3},{5,4},{6,5},{7,6},{8,7},{9,8},{10,9},{11,1... | collective-permute-start | bytes 552968 | tf_op jit(solution)/shard_map/ppermute | solution.py:358
  34.4 1.9 collective-permute-start.4
  36.3 0.4 fusion.2
  36.7 0.7 pad_add_fusion.1.counts_ref
  37.4 9.1 %near_3.1.refs_0_ = f32[4,8,256]{2,1,0:T(8,128)S(1)} custom-call(s32[22]{0:T(128)S(1)} %pad_add_fusion.1.counts_ref, f32[180,256]{1,0:T(8,128)S(1)} %concatenate.22.refs_0_, f32[4,10,256]{2,1,0:T(8,128)S(1)} %maximum_bitcast_fusion.refs_1_.refs_2_.own_ref), custom_call_target="tpu_custom_call" | custom-call | tf_op jit(solution)/shard_map/near_3/pallas_call | solution.py:268
  46.5 0.0 collective-permute-done.5.refs_1_
  46.6 0.0 collective-permute-done.4.refs_0_
  46.6 0.4 fusion
  47.0 0.4 fusion.1
  47.4 0.0 copy-done.1
  47.5 0.1 pad_add_fusion.2.counts_ref
  47.5 13.4 %near_6.1.refs_1_ = f32[4,8,256]{2,1,0:T(8,128)S(1)} custom-call(s32[40]{0:T(128)S(1)} %pad_add_fusion.2.counts_ref, f32[180,256]{1,0:T(8,128)S(1)} %collective-permute-done.4.refs_0_, f32[180,256]{1,0:T(8,128)S(1)} %collective-permute-done.5.refs_1_, f32[4,10,256]{2,1,0:T(8,128)S(1)} %maximum_bitcast_fusion.refs_1_.refs_2_.own_ref), custom_call_target="tpu_custom_call" | custom-call | tf_op jit(solution)/shard_map/near_6/pallas_call | solution.py:268
  61.0 150.5 %all-gather.2.cloned.1.call-done = f32[4096,128]{1,0:T(8,128)} async-done(((f32[8,128]{1,0:T(8,128)}), f32[4096,128]{1,0:T(8,128)}) %all-gather.2.cloned.1.call-update) | async-done | bytes 2097168 | tf_op jit(solution)/shard_map/all_gather | solution.py:402
  211.4 1.7 slice.32
  213.2 0.0 copy-done
  213.2 1.0 far.1
  214.2 0.6 copy.35
  (10 shorter events, 0.2 us)
Async XLA Ops:
  6.5 40.9 %copy-start.1 = (s32[4,1,1]{0,2,1:T(1,128)S(1)}, s32[4,1,1]{0,2,1:T(1,128)}, u32[]{:S(2)}) copy-start(s32[4,1,1]{0,2,1:T(1,128)} %param.8) | copy-start | bytes 52
  6.5 206.6 %copy-start = (f32[3,3]{1,0:T(4,128)S(1)}, f32[3,3]{1,0:T(4,128)}, u32[]{:S(2)}) copy-start(f32[3,3]{1,0:T(4,128)} %applied_ref.1) | copy-start | bytes 112
  6.5 204.9 %all-gather.2.cloned.1.call-start = ((), (), s32[]{:S(2)}) async-start(), calls=%async_computation | async-start | bytes 2101248 | tf_op jit(solution)/shard_map/all_gather | solution.py:402
  10.4 6.0 %collective-permute-start.1 = (f32[10,256]{1,0:T(8,128)S(1)}, f32[10,256]{1,0:T(8,128)S(1)}, u32[]{:S(2)}, u32[]{:S(2)}) collective-permute-start(f32[10,256]{1,0:T(8,128)S(1)} %get-tuple-element.6), channel_id=1, source_target_pairs={{128,0},{256,128},{384,256},{129,1},{257,129},{385,257},{130,2},{2... | collective-permute-start | bytes 30728 | tf_op jit(solution)/shard_map/ppermute | solution.py:358
  11.7 5.5 %collective-permute-start = (f32[10,256]{1,0:T(8,128)S(1)}, f32[10,256]{1,0:T(8,128)S(1)}, u32[]{:S(2)}, u32[]{:S(2)}) collective-permute-start(f32[10,256]{1,0:T(8,128)S(1)} %get-tuple-element.5), channel_id=1, source_target_pairs={{0,128},{128,256},{256,384},{1,129},{129,257},{257,385},{2,130},{1... | collective-permute-start | bytes 30728 | tf_op jit(solution)/shard_map/ppermute | solution.py:358
  17.2 4.7 %collective-permute-start.2 = (f32[60,256]{1,0:T(8,128)S(1)}, f32[60,256]{1,0:T(8,128)S(1)}, u32[]{:S(2)}, u32[]{:S(2)}) collective-permute-start(f32[60,256]{1,0:T(8,128)S(1)} %pad_maximum_fusion), channel_id=1, source_target_pairs={{0,32},{32,64},{64,96},{1,33},{33,65},{65,97},{2,34},{34,66},{66,9... | collective-permute-start | bytes 184328 | tf_op jit(solution)/shard_map/ppermute | solution.py:358
  20.5 5.0 %collective-permute-start.3 = (f32[60,256]{1,0:T(8,128)S(1)}, f32[60,256]{1,0:T(8,128)S(1)}, u32[]{:S(2)}, u32[]{:S(2)}) collective-permute-start(f32[60,256]{1,0:T(8,128)S(1)} %pad_maximum_fusion), channel_id=1, source_target_pairs={{32,0},{64,32},{96,64},{33,1},{65,33},{97,65},{34,2},{66,34},{98,6... | collective-permute-start | bytes 184328 | tf_op jit(solution)/shard_map/ppermute | solution.py:358
  25.9 20.6 %collective-permute-start.5 = (f32[180,256]{1,0:T(8,128)S(1)}, f32[180,256]{1,0:T(8,128)S(1)}, u32[]{:S(2)}, u32[]{:S(2)}) collective-permute-start(f32[180,256]{1,0:T(8,128)S(1)} %concatenate.22.refs_0_), channel_id=1, source_target_pairs={{1,0},{2,1},{3,2},{4,3},{5,4},{6,5},{7,6},{8,7},{9,8},{10,9},{11,1... | collective-permute-start | bytes 552968 | tf_op jit(solution)/shard_map/ppermute | solution.py:358
  34.4 12.2 %collective-permute-start.4 = (f32[180,256]{1,0:T(8,128)S(1)}, f32[180,256]{1,0:T(8,128)S(1)}, u32[]{:S(2)}, u32[]{:S(2)}) collective-permute-start(f32[180,256]{1,0:T(8,128)S(1)} %concatenate.22.refs_0_), channel_id=1, source_target_pairs={{0,1},{1,2},{2,3},{3,4},{4,5},{5,6},{6,7},{7,8},{8,9},{9,10},{10,1... | collective-permute-start | bytes 552968 | tf_op jit(solution)/shard_map/ppermute | solution.py:358
Sparse Core Ops, SparseCore 0:
  11.9 199.4 all-gather.1

commit v2 on v1

--- a/solution.py
+++ b/solution.py
@@ -100,42 +100,43 @@
     return out
 
 
-def near_kernel(planes, offsets, counts_ref, *refs):
-    sources = refs[: len(offsets)]
-    refs = refs[len(offsets):]
-    own_ref, out_ref = refs[:2]
-    raw, feat, wide, left3, left5, live_ref = refs[2:]
-    columns = [(k, c, d) for k, group in enumerate(offsets) for c, d in enumerate(group)]
+def near_kernel(planes, before_ref, middle_ref, after_ref, total, raw, feat, wide, left3, left5, own, live_ref, own_live):
+    sources = (before_ref, middle_ref, after_ref)
+    cells = planes - 2
+    columns = [(k, c) for k in range(3) for c in range(3)]
     blocks = -(-(2 * len(columns) + 1) // 8) * 8
-    chunks = blocks // 2
     lane = lax.broadcasted_iota(jnp.int32, (ROWS, LANES), 1)
     lift = lax.broadcasted_iota(jnp.int32, (ROWS, LANES), 0)
-
     raw[...] = jnp.zeros_like(raw)
     feat[...] = jnp.zeros_like(feat)
-    out_ref[...] = jnp.zeros_like(out_ref)
+    total[...] = jnp.zeros_like(total)
 
     for j in range(planes):
         at = jnp.int32(0)
-        for k, c, (dy, dz) in columns:
-            cell = c * planes + j
+        for k, c in columns:
+            row = ROWS * (c * planes + j)
             shift = (
                 jnp.where(lift < 3, -0.5, 0.0)
-                + jnp.where(lift == 1, float(dy), 0.0)
-                + jnp.where(lift == 2, float(dz), 0.0)
+                + jnp.where(lift == 1, float(c - 1), 0.0)
+                + jnp.where(lift == 2, float(k - 1), 0.0)
             )
-            first = sources[k][ROWS * cell: ROWS * cell + ROWS, 0:LANES] + shift
-            second = sources[k][ROWS * cell: ROWS * cell + ROWS, LANES:] + shift
+            first = sources[k][row: row + ROWS, 0:LANES]
+            second = sources[k][row: row + ROWS, LANES:]
+            count = first[ROWS - 1: ROWS, 0:1].astype(jnp.int32)[0, 0]
+            if k == 1 and c == 1 and 0 < j < planes - 1:
+                own[j - 1, 0:ROWS, 0:LANES] = first
+                own[j - 1, 0:ROWS, LANES:] = second
+                own_live[j - 1] = count
             low = jnp.bitwise_and(at, LANES - 1)
             base = lax.shift_right_logical(at, 7) + j * blocks
-            first = pltpu.roll(first, low, 1)
-            second = pltpu.roll(second, low, 1)
+            first = pltpu.roll(first + shift, low, 1)
+            second = pltpu.roll(second + shift, low, 1)
             keep = lane >= low
             place = pl.multiple_of(base * 16, 16)
             raw[pl.ds(place, ROWS), :] = jnp.where(keep, first, raw[pl.ds(place, ROWS), :])
             raw[pl.ds(place + 16, ROWS), :] = jnp.where(keep, second, first)
             raw[pl.ds(place + 32, ROWS), :] = jnp.where(keep, 0.0, second)
-            at = at + counts_ref[k * len(offsets[k]) * planes + cell]
+            at = at + count
         live_ref[j] = at
 
     def plane_body(j, carry):
@@ -151,19 +152,24 @@
                 feat[pl.ds(r, 8, stride=NUM3 + NUM5), :] = value
             for r, value in rows5.items():
                 feat[pl.ds(NUM3 + r, 8, stride=NUM3 + NUM5), :] = value
-            for q in range(8):
-                piece = halves(feat[q * 80: q * 80 + NUM3, :], 3)
-                span = slice((q % 2) * LANES, (q % 2 + 1) * LANES)
-                for n in range(3):
-                    left3[g * 4 + q // 2, n * NUM3: (n + 1) * NUM3, span] = piece[n]
-                piece = halves(feat[q * 80 + NUM3: (q + 1) * 80, :], 3)
-                for n in range(3):
-                    left5[g * 4 + q // 2, n * NUM5: (n + 1) * NUM5, span] = piece[n]
-                turned = jnp.transpose(raw[pl.ds(start + q * 16, 8), :])
-                for n in range(3):
-                    wide[g * 4 + q // 2, n, (q % 2) * LANES: (q % 2 + 1) * LANES, :] = (
-                        jnp.broadcast_to(turned[:, n: n + 1], (LANES, LANES))
-                    )
+
+            def chunk_body(c, carry):
+                for h in range(2):
+                    q = (c - g * 4) * 2 + h
+                    span = slice(h * LANES, (h + 1) * LANES)
+                    at = pl.multiple_of(q * (NUM3 + NUM5), 16)
+                    piece = halves(feat[pl.ds(at, NUM3), :], 3)
+                    for n in range(3):
+                        left3[c, n * NUM3: (n + 1) * NUM3, span] = piece[n]
+                    piece = halves(feat[pl.ds(at + NUM3, NUM5), :], 3)
+                    for n in range(3):
+                        left5[c, n * NUM5: (n + 1) * NUM5, span] = piece[n]
+                    turned = jnp.transpose(raw[pl.ds(pl.multiple_of(start + q * 16, 16), 8), :])
+                    for n in range(3):
+                        wide[c, n, span, :] = jnp.broadcast_to(turned[:, n: n + 1], (LANES, LANES))
+                return carry
+
+            lax.fori_loop(g * 4, jnp.minimum(g * 4 + 4, steps), chunk_body, 0)
             return carry
 
         lax.fori_loop(0, groups, group_body, 0)
@@ -171,11 +177,11 @@
         def cell_body(i, carry):
             where_x = (i + 1 - j).astype(jnp.float32) - 0.5
             points = [
-                own_ref[i, 0:1, :] + where_x,
-                own_ref[i, 1:2, :] - 0.5,
-                own_ref[i, 2:3, :] - 0.5,
+                own[i, 0:1, :] + where_x,
+                own[i, 1:2, :] - 0.5,
+                own[i, 2:3, :] - 0.5,
             ]
-            targets = counts_ref[counts_ref.shape[0] - 4 + i]
+            targets = own_live[i]
 
             def run(parts):
                 width = parts * LANES
@@ -242,7 +248,7 @@
                 )
                 v = [v[n] + scale * x[n] for n in range(3)]
                 for n, (a, b) in enumerate(PAIRS):
-                    out_ref[i, n: n + 1, 0:width] += linear[n: n + 1] + x[a] * v[b] + x[b] * v[a]
+                    total[i, n: n + 1, 0:width] += linear[n: n + 1] + x[a] * v[b] + x[b] * v[a]
 
             @pl.when(targets > LANES)
             def _():
@@ -260,42 +266,17 @@
     lax.fori_loop(0, planes, plane_body, 0)
 
 
-def near(planes, offsets, counts, sources, own):
-    columns = sum(len(group) for group in offsets)
-    blocks = -(-(2 * columns + 1) // 8) * 8
+def far_kernel(planes, spans, place_ref, moment_ref, applied_ref, sheet_ref, total, out_ref):
     cells = planes - 2
-    vmem = pl.BlockSpec(memory_space=pltpu.VMEM)
-    return pl.pallas_call(
-        functools.partial(near_kernel, planes, offsets),
-        out_shape=jax.ShapeDtypeStruct((cells, 8, CAP), jnp.float32),
-        in_specs=[pl.BlockSpec(memory_space=pltpu.SMEM)] + [vmem] * (len(sources) + 1),
-        out_specs=vmem,
-        scratch_shapes=[
-            pltpu.VMEM((planes * blocks * 16, LANES), jnp.float32),
-            pltpu.VMEM((8 * (NUM3 + NUM5), LANES), jnp.float32),
-            pltpu.VMEM((blocks // 2, 3, CAP, LANES), jnp.float32),
-            pltpu.VMEM((blocks // 2, 3 * NUM3, CAP), jnp.bfloat16),
-            pltpu.VMEM((blocks // 2, 3 * NUM5, CAP), jnp.bfloat16),
-            pltpu.SMEM((planes,), jnp.int32),
-        ],
-        compiler_params=pltpu.CompilerParams(vmem_limit_bytes=32 * 1024 * 1024),
-        name="near_%d" % columns,
-    )(counts, *sources, own)
-
-
-def far_kernel(spans, moment_ref, place_ref, applied_ref, own_ref, *refs):
-    parts, out_ref = refs[:-1], refs[-1]
-    span_y, span_z = spans
-    cells = own_ref.shape[0]
-    count = moment_ref.shape[0]
-    turned = jnp.transpose(moment_ref[...])
-    moment = [turned[cells * m: cells * m + cells, :] for m in range(9)]
-    device = lax.broadcasted_iota(jnp.int32, (cells, count), 1)
-    inner = lax.broadcasted_iota(jnp.int32, (cells, count), 0)
+    span_x, span_y, span_z = spans
+    shape = (span_z, LANES)
+    moment = [moment_ref[pl.ds(m, span_z, stride=16), :] for m in range(9)]
+    column = lax.broadcasted_iota(jnp.int32, shape, 1)
+    device = column // cells
     source = (
-        (device // (span_y * span_z) * cells + inner).astype(jnp.float32),
-        (device // span_z % span_y).astype(jnp.float32),
-        (device % span_z).astype(jnp.float32),
+        (device // span_y * cells + column % cells).astype(jnp.float32),
+        (device % span_y).astype(jnp.float32),
+        lax.broadcasted_iota(jnp.int32, shape, 0).astype(jnp.float32),
     )
     w = (moment[5] - moment[7], moment[6] - moment[2], moment[1] - moment[3])
     index = {}
@@ -328,79 +309,112 @@
             stress.append(
                 jnp.sum(element, axis=(0, 1), keepdims=True)
                 + 0.5 * (applied_ref[a, b] + applied_ref[b, a])
-                + plus([part[i, n: n + 1, :] for part in parts])
+                + total[i, n: n + 1, :]
             )
-        t = [own_ref[i, 3 + n: 4 + n, :] for n in range(3)]
-        b = [own_ref[i, 6 + n: 7 + n, :] for n in range(3)]
+        row = ROWS * (planes + 1 + i)
+        t = [sheet_ref[row + 3 + n: row + 4 + n, :] for n in range(3)]
+        b = [sheet_ref[row + 6 + n: row + 7 + n, :] for n in range(3)]
         force = [plus([stress[index[m, n]] * b[n] for n in range(3)]) for m in range(3)]
         for n, value in enumerate(cross(force, t)):
             out_ref[n, i: i + 1, :] = value
 
 
-def far(spans, moments, place, applied, own, parts):
-    cells = own.shape[0]
-    vmem = pl.BlockSpec(memory_space=pltpu.VMEM)
-    smem = pl.BlockSpec(memory_space=pltpu.SMEM)
-    return pl.pallas_call(
-        functools.partial(far_kernel, spans),
-        out_shape=jax.ShapeDtypeStruct((3, cells, CAP), jnp.float32),
-        in_specs=[vmem, smem, smem, vmem] + [vmem] * len(parts),
-        out_specs=vmem,
-        compiler_params=pltpu.CompilerParams(vmem_limit_bytes=32 * 1024 * 1024),
-        name="far",
-    )(moments, place, applied, own, *parts)
-
-
-def beside(first, last, axis):
-    devices = lax.axis_size(axis)
-    up = [(i, i + 1) for i in range(devices - 1)]
-    down = [(i + 1, i) for i in range(devices - 1)]
-    return lax.ppermute(last, axis, up), lax.ppermute(first, axis, down)
+def pick_kernel(planes, spans, place_ref, all_ref, sheet_ref, moment_ref):
+    span_x, span_y, span_z = spans
+    cells = planes - 2
+    for dy in range(3):
+        y = place_ref[1] + (dy - 1)
+        for j in range(planes):
+            step = (j + cells - 1) // cells - 1
+            c = (j - 1) % cells
+            x = place_ref[0] + step
+            inside = (x >= 0) & (x < span_x) & (y >= 0) & (y < span_y)
+            device = jnp.clip(x, 0, span_x - 1) * span_y + jnp.clip(y, 0, span_y - 1)
+            row = ROWS * (dy * planes + j)
+            sheet_ref[row: row + ROWS, :] = jnp.where(
+                inside, all_ref[device, ROWS * c: ROWS * c + ROWS, :], 0.0
+            )
+    rows = [
+        all_ref[d, ROWS * c + ROWS - 1: ROWS * c + ROWS, LANES:]
+        for d in range(span_x * span_y)
+        for c in range(cells)
+    ]
+    rows.append(jnp.zeros((LANES - len(rows), LANES), jnp.float32))
+    moment_ref[...] = jnp.transpose(jnp.concatenate(rows, axis=0))[0:16, :]
 
 
 def local(seg_offset, seg_vector, burgers, cell_counts, applied):
     cells = seg_offset.shape[1]
     planes = cells + 2
+    spans = tuple(lax.axis_size(a) for a in ("gx", "gy", "gz"))
+    place = jnp.stack([lax.axis_index(a) for a in ("gx", "gy", "gz")]).astype(jnp.int32)
     counts = cell_counts.reshape(cells)
     slots = jnp.arange(CAP, dtype=jnp.int32)
     filled = slots[None, :] < counts[:, None]
     offset = seg_offset.reshape(3, cells, CAP)
     tangent = jnp.where(filled[None], seg_vector.reshape(3, cells, CAP), 0.0)
     charge = jnp.where(filled[None], burgers.reshape(3, cells, CAP), 0.0)
-    moment = jnp.sum(charge[:, None] * tangent[None, :], axis=-1).reshape(1, 9 * cells)
-    moments = gathered(jnp.pad(moment, ((0, 0), (0, LANES - 9 * cells))))
-    level = jnp.broadcast_to(counts.astype(jnp.float32)[None, :, None], (1, cells, CAP))
-    own = jnp.concatenate([offset, tangent, charge, level]).transpose(1, 0, 2)
-    flat = own.reshape(cells * ROWS, CAP)
-    before, after = beside(flat[:ROWS], flat[-ROWS:], "gx")
-    column = jnp.concatenate([before, flat, after])
-    before, after = beside(column, column, "gy")
-    sheet = jnp.concatenate([before, column, after])
-    before, after = beside(sheet, sheet, "gz")
-
-    def live(array):
-        return array.reshape(-1, ROWS, CAP)[:, ROWS - 1, 0].astype(jnp.int32)
-
-    middle = [(dy, 0) for dy in (-1, 0, 1)]
-    outer = [[(dy, dz) for dy in (-1, 0, 1)] for dz in (-1, 1)]
-    near_a = near(planes, [middle], jnp.concatenate([live(sheet), counts]), [sheet], own)
-    near_b = near(
-        planes,
-        outer,
-        jnp.concatenate([live(before), live(after), counts]),
-        [before, after],
-        own,
+    moment = jnp.sum(charge[:, None] * tangent[None, :], axis=-1).reshape(9, cells).T
+    level = jnp.broadcast_to(counts.astype(jnp.float32)[:, None], (cells, LANES))
+    level = jnp.concatenate([level, moment, jnp.zeros((cells, LANES - 9), jnp.float32)], axis=1)
+    packed = jnp.concatenate([offset, tangent, charge, level[None]]).transpose(1, 0, 2)
+    packed = packed.reshape(cells * ROWS, CAP)
+
+    devices = spans[0] * spans[1]
+    every = lax.all_to_all(
+        jnp.broadcast_to(packed[None], (devices,) + packed.shape), ("gx", "gy"), 0, 0
     )
-    place = jnp.stack([lax.axis_index(a) for a in ("gx", "gy", "gz")]).astype(jnp.int32)
-    spans = (lax.axis_size("gy"), lax.axis_size("gz"))
-    result = far(spans, moments, place, applied, own, [near_a, near_b])
+    vmem = pl.BlockSpec(memory_space=pltpu.VMEM)
+    smem = pl.BlockSpec(memory_space=pltpu.SMEM)
+    limit = pltpu.CompilerParams(vmem_limit_bytes=40 * 1024 * 1024)
+    sheet, moments = pl.pallas_call(
+        functools.partial(pick_kernel, planes, spans),
+        out_shape=(
+            jax.ShapeDtypeStruct((3 * planes * ROWS, CAP), jnp.float32),
+            jax.ShapeDtypeStruct((16, LANES), jnp.float32),
+        ),
+        in_specs=[smem, vmem],
+        out_specs=(vmem, vmem),
+        compiler_params=limit,
+        name="pick",
+    )(place, every)
+    up = [(i, i + 1) for i in range(spans[2] - 1)]
+    down = [(i + 1, i) for i in range(spans[2] - 1)]
+    before = lax.ppermute(sheet, "gz", up)
+    after = lax.ppermute(sheet, "gz", down)
+    moments = lax.all_to_all(
+        jnp.broadcast_to(moments[None], (spans[2],) + moments.shape), "gz", 0, 0
+    ).reshape(spans[2] * 16, LANES)
+
+    blocks = 24
+    total = pl.pallas_call(
+        functools.partial(near_kernel, planes),
+        out_shape=jax.ShapeDtypeStruct((cells, 8, CAP), jnp.float32),
+        in_specs=[vmem, vmem, vmem],
+        out_specs=vmem,
+        scratch_shapes=[
+            pltpu.VMEM((planes * blocks * 16, LANES), jnp.float32),
+            pltpu.VMEM((8 * (NUM3 + NUM5), LANES), jnp.float32),
+            pltpu.VMEM((blocks // 2, 3, CAP, LANES), jnp.float32),
+            pltpu.VMEM((blocks // 2, 3 * NUM3, CAP), jnp.bfloat16),
+            pltpu.VMEM((blocks // 2, 3 * NUM5, CAP), jnp.bfloat16),
+            pltpu.VMEM((cells, 16, CAP), jnp.float32),
+            pltpu.SMEM((planes,), jnp.int32),
+            pltpu.SMEM((cells,), jnp.int32),
+        ],
+        compiler_params=limit,
+        cost_estimate=pl.CostEstimate(flops=10**9, bytes_accessed=10**7, transcendentals=0),
+        name="near",
+    )(before, sheet, after)
+    result = pl.pallas_call(
+        functools.partial(far_kernel, planes, spans),
+        out_shape=jax.ShapeDtypeStruct((3, cells, CAP), jnp.float32),
+        in_specs=[smem, vmem, smem, vmem, vmem],
+        out_specs=vmem,
+        compiler_params=limit,
+        name="far",
+    )(place, moments, applied, sheet, total)
     return result.reshape(seg_offset.shape)
-
-
-def gathered(moment):
-    wide = jnp.concatenate([moment] * 8, axis=0)
-    whole = lax.all_gather(wide, ("gx", "gy", "gz"), axis=0, tiled=True)
-    return whole.reshape(-1, 8, LANES)[:, 0, :]
 
 
 def solution(mesh):

time: 222 us -> 77.4 us (0.35)
  the two profiles are of different devices: /device:TPU:1 before, /device:TPU:435 now
where the time goes in v2:
time: 77.4 us; the launch traced here: 76.8 us
  Pallas kernels  29.9 us (39%)
  starting transfers between devices  22.8 us (29%)
  waiting for transfers between devices  18.7 us (24%)
  local copies, waits for them, and re-layouts  3.73 us (5%)
  other arithmetic  1.66 us (2%)
    pallas_call x1, Pallas kernels, local(): pl.pallas_call(functools.partial(near_kernel, planes), out_shape=jax.Shap...  28.3 us
    all_to_all x1, starting transfers between devices, local(): lax.all_to_all(jnp.broadcast_to(moments[None], (spans[2],) + moments.shap...  11.7 us
    all_to_all x1, waiting for transfers between devices, local(): lax.all_to_all(jnp.broadcast_to(packed[None], (devices,) + packed.shape),...  8.5 us
    ppermute x1, waiting for transfers between devices, local(): before = lax.ppermute(sheet, 'gz', up)  8.24 us
    all_to_all x1, starting transfers between devices, local(): lax.all_to_all(jnp.broadcast_to(packed[None], (devices,) + packed.shape),...  6.69 us
    ppermute x1, starting transfers between devices, local(): before = lax.ppermute(sheet, 'gz', up)  2.45 us
    ppermute x1, starting transfers between devices, local(): after = lax.ppermute(sheet, 'gz', down)  1.92 us
    ppermute x1, waiting for transfers between devices, local(): after = lax.ppermute(sheet, 'gz', down)  1.91 us
  transfers between devices with their start and end apart: 4, of which 3 were waited for; matrix products, arithmetic and copies ran while one was open for 0% of the time, Pallas kernels for 37%

profile of v2, /device:TPU:435, one launch (start us, length us, event | category | flops | bytes accessed | tf_op | source)
XLA Modules:
  0.0 76.8 jit_solution(16863410454024552535)
XLA Ops:
  0.0 0.7 bitcast_convert_fusion
  0.7 0.0 copy-start.2
  0.7 0.7 copy-done.2
  1.3 0.1 iota_compare_fusion
  1.4 0.7 bitcast_select_fusion
  2.1 0.1 multiply_reduce_fusion
  2.2 0.0 copy-start.1
  2.2 0.1 copy.12
  2.3 0.6 copy-done.1
  2.9 0.1 pad.6.clone
  3.0 0.1 broadcast_in_dim.48
  3.1 0.9 %broadcast_in_dim.52 = f32[16,40,256]{2,1,0:T(8,128)} broadcast(f32[40,256]{1,0:T(8,128)S(1)} %broadcast_in_dim.51), dimensions={1,2} | broadcast | bytes 696320 | tf_op jit(solution)/shard_map/broadcast_in_dim | solution.py:365
  4.0 6.7 %all-to-all-start = ((f32[16,40,256]{2,1,0:T(8,128)}), f32[16,40,256]{2,1,0:T(8,128)S(1)}, u32[]{:S(2)}, u32[]{:S(2)}) async-start(f32[16,40,256]{2,1,0:T(8,128)} %broadcast_in_dim.52), calls=%async_computation | async-start | bytes 1310720 | tf_op jit(solution)/shard_map/all_to_all | solution.py:364
  10.7 0.1 pad_add_fusion.place_ref
  10.8 8.5 %all-to-all-done.all_ref = f32[16,40,256]{2,1,0:T(8,128)S(1)} async-done(((f32[16,40,256]{2,1,0:T(8,128)}), f32[16,40,256]{2,1,0:T(8,128)S(1)}, u32[]{:S(2)}, u32[]{:S(2)}) %all-to-all-start) | async-done | bytes 655392 | tf_op jit(solution)/shard_map/all_to_all | solution.py:364
  19.3 0.6 pick.1
  19.9 0.7 broadcast_in_dim.53
  20.6 11.7 %all-to-all-start.1 = ((f32[32,16,128]{2,1,0:T(8,128)}), f32[32,16,128]{2,1,0:T(8,128)S(1)}, u32[]{:S(2)}, u32[]{:S(2)}) async-start(f32[32,16,128]{2,1,0:T(8,128)} %broadcast_in_dim.53), calls=%async_computation.1 | async-start | bytes 524288 | tf_op jit(solution)/shard_map/all_to_all | solution.py:385
  32.4 2.5 %collective-permute-start = (f32[180,256]{1,0:T(8,128)S(1)}, f32[180,256]{1,0:T(8,128)S(1)}, u32[]{:S(2)}, u32[]{:S(2)}) collective-permute-start(f32[180,256]{1,0:T(8,128)S(1)} %get-tuple-element.8.middle_ref.sheet_ref), channel_id=1, source_target_pairs={{0,1},{1,2},{2,3},{3,4},{4,5},{5,6},{6,7},{7,8},{8,9},{9,10},{10,1... | collective-permute-start | bytes 552968 | tf_op jit(solution)/shard_map/ppermute | solution.py:383
  34.8 1.9 %collective-permute-start.1 = (f32[180,256]{1,0:T(8,128)S(1)}, f32[180,256]{1,0:T(8,128)S(1)}, u32[]{:S(2)}, u32[]{:S(2)}) collective-permute-start(f32[180,256]{1,0:T(8,128)S(1)} %get-tuple-element.8.middle_ref.sheet_ref), channel_id=1, source_target_pairs={{1,0},{2,1},{3,2},{4,3},{5,4},{6,5},{7,6},{8,7},{9,8},{10,9},{11,1... | collective-permute-start | bytes 552968 | tf_op jit(solution)/shard_map/ppermute | solution.py:384
  36.7 8.2 %collective-permute-done.before_ref = f32[180,256]{1,0:T(8,128)S(1)} collective-permute-done((f32[180,256]{1,0:T(8,128)S(1)}, f32[180,256]{1,0:T(8,128)S(1)}, u32[]{:S(2)}, u32[]{:S(2)}) %collective-permute-start) | collective-permute-done | bytes 184352 | tf_op jit(solution)/shard_map/ppermute | solution.py:383
  45.0 1.9 %collective-permute-done.1.after_ref = f32[180,256]{1,0:T(8,128)S(1)} collective-permute-done((f32[180,256]{1,0:T(8,128)S(1)}, f32[180,256]{1,0:T(8,128)S(1)}, u32[]{:S(2)}, u32[]{:S(2)}) %collective-permute-start.1) | collective-permute-done | bytes 184352 | tf_op jit(solution)/shard_map/ppermute | solution.py:384
  46.9 0.0 copy-start
  46.9 28.3 %near.1.total = f32[4,8,256]{2,1,0:T(8,128)S(1)} custom-call(f32[180,256]{1,0:T(8,128)S(1)} %collective-permute-done.before_ref, f32[180,256]{1,0:T(8,128)S(1)} %get-tuple-element.8.middle_ref.sheet_ref, f32[180,256]{1,0:T(8,128)S(1)} %collective-permute-done.1.after_ref), custom_call_target="tpu_custom_call" | custom-call | flops 1000000000 | bytes 10000000 | tf_op jit(solution)/shard_map/near/pallas_call | solution.py:390
  75.2 0.0 all-to-all-done.1
  75.2 0.0 copy-done
  75.3 1.0 %far.1 = f32[3,4,256]{2,1,0:T(4,128)S(1)} custom-call(s32[3]{0:T(128)S(1)} %pad_add_fusion.place_ref, f32[512,128]{1,0:T(8,128)S(1)} %bitcast.19, f32[3,3]{1,0:T(4,128)S(1)} %copy-done, f32[180,256]{1,0:T(8,128)S(1)} %get-tuple-element.8.middle_ref.sheet_ref, f32[4,8,256]{2,1,0:T(8,128)S(1)} %near.1.total), custom_call_target="tpu_custom_call" | custom-call | tf_op jit(solution)/shard_map/far/pallas_call | solution.py:409
  76.2 0.6 copy.11
  (7 shorter events, 0.1 us)
Async XLA Ops:
  0.7 0.7 copy-start.2
  2.2 0.7 copy-start.1
  4.0 15.3 %all-to-all-start = ((f32[16,40,256]{2,1,0:T(8,128)}), f32[16,40,256]{2,1,0:T(8,128)S(1)}, u32[]{:S(2)}, u32[]{:S(2)}) async-start(f32[16,40,256]{2,1,0:T(8,128)} %broadcast_in_dim.52), calls=%async_computation | async-start | bytes 1310720 | tf_op jit(solution)/shard_map/all_to_all | solution.py:364
  20.6 54.6 %all-to-all-start.1 = ((f32[32,16,128]{2,1,0:T(8,128)}), f32[32,16,128]{2,1,0:T(8,128)S(1)}, u32[]{:S(2)}, u32[]{:S(2)}) async-start(f32[32,16,128]{2,1,0:T(8,128)} %broadcast_in_dim.53), calls=%async_computation.1 | async-start | bytes 524288 | tf_op jit(solution)/shard_map/all_to_all | solution.py:385
  32.4 12.6 %collective-permute-start = (f32[180,256]{1,0:T(8,128)S(1)}, f32[180,256]{1,0:T(8,128)S(1)}, u32[]{:S(2)}, u32[]{:S(2)}) collective-permute-start(f32[180,256]{1,0:T(8,128)S(1)} %get-tuple-element.8.middle_ref.sheet_ref), channel_id=1, source_target_pairs={{0,1},{1,2},{2,3},{3,4},{4,5},{5,6},{6,7},{7,8},{8,9},{9,10},{10,1... | collective-permute-start | bytes 552968 | tf_op jit(solution)/shard_map/ppermute | solution.py:383
  34.8 12.1 %collective-permute-start.1 = (f32[180,256]{1,0:T(8,128)S(1)}, f32[180,256]{1,0:T(8,128)S(1)}, u32[]{:S(2)}, u32[]{:S(2)}) collective-permute-start(f32[180,256]{1,0:T(8,128)S(1)} %get-tuple-element.8.middle_ref.sheet_ref), channel_id=1, source_target_pairs={{1,0},{2,1},{3,2},{4,3},{5,4},{6,5},{7,6},{8,7},{9,8},{10,9},{11,1... | collective-permute-start | bytes 552968 | tf_op jit(solution)/shard_map/ppermute | solution.py:384
  46.9 28.4 %copy-start = (f32[3,3]{1,0:T(4,128)S(1)}, f32[3,3]{1,0:T(4,128)}, u32[]{:S(2)}) copy-start(f32[3,3]{1,0:T(4,128)} %applied_ref.1) | copy-start | bytes 112

commit v3 on v2

v3 whole, which is shorter than its diff:
```python
import functools
import math

import jax
import jax.numpy as jnp
from jax import lax
from jax.experimental import pallas as pl
from jax.experimental.pallas import tpu as pltpu
from jax.sharding import PartitionSpec as P

CORE_SQUARE = 0.2 * 0.2
FIRST = 1.0 / (8.0 * math.pi)
SECOND = 1.0 / (4.0 * math.pi * 0.7)
KAPPA = 3.0 * CORE_SQUARE
CAP = 256
LANES = 128
ROWS = 10
PAIRS = ((0, 0), (0, 1), (0, 2), (1, 1), (1, 2), (2, 2))
NUM3 = 32
NUM5 = 48
BLOCKS = 24
CHUNKS = 9
TILES = 4


def cross(a, b):
    return (
        a[1] * b[2] - a[2] * b[1],
        a[2] * b[0] - a[0] * b[2],
        a[0] * b[1] - a[1] * b[0],
    )


def plus(terms):
    terms = [t for t in terms if t is not None]
    total = terms[0]
    for t in terms[1:]:
        total = total + t
    return total


def features(y, t, b):
    w = cross(b, t)
    turn = [[None, b[2], -b[1]], [-b[2], None, b[0]], [b[1], -b[0], None]]
    c2w = [SECOND * v for v in w]
    lin3, lin5 = {}, {}
    for n, (i, j) in enumerate(PAIRS):
        for m in range(3):
            parts = []
            if turn[i][m] is not None:
                parts.append(turn[i][m] * t[j])
            if turn[j][m] is not None:
                parts.append(turn[j][m] * t[i])
            base = plus(parts) * (-FIRST) if parts else None
            a3 = [2.0 * base] if base is not None else []
            a5 = [base] if base is not None else []
            if i == j:
                a3.append(c2w[m])
                a5.append(c2w[m])
            if m == j:
                a3.append(-c2w[i])
            if m == i:
                a3.append(-c2w[j])
            lin3[m, n] = plus(a3) if a3 else None
            lin5[m, n] = KAPPA * plus(a5) if a5 else None
    w3 = [3.0 * v for v in c2w]
    wy = [[w3[m] * y[n] for n in range(3)] for m in range(3)]
    dot = wy[0][0] + wy[1][1] + wy[2][2]
    doty = [dot * y[n] for n in range(3)]
    rows3, rows5 = {}, {}
    for n, (i, j) in enumerate(PAIRS):
        zero3, zero5 = [], [doty[i] * y[j]]
        for m in range(3):
            if lin3[m, n] is not None:
                rows3[8 * m + n] = lin3[m, n]
                zero3.append(lin3[m, n] * y[m])
            quad = [wy[m][i] * y[j]]
            if m == i:
                quad.append(doty[j])
            if m == j:
                quad.append(doty[i])
            if lin5[m, n] is not None:
                quad.append(lin5[m, n])
                zero5.append(lin5[m, n] * y[m])
            rows5[8 * m + n] = plus(quad)
        if zero3:
            rows3[24 + n] = -plus(zero3)
        rows5[24 + n] = -plus(zero5)
    for m in range(3):
        for n in range(3):
            rows5[32 + 3 * m + n] = -wy[m][n]
        rows5[41 + m] = w3[m]
    return rows3, rows5


def halves(value, terms):
    out = []
    for k in range(terms):
        part = value.astype(jnp.bfloat16)
        out.append(part)
        if k + 1 < terms:
            value = value - part.astype(jnp.float32)
    return out


def near_kernel(
    planes, before_ref, middle_ref, after_ref, out_ref,
    raw, feat, cols, left3, left5, left_d, right_d, line,
    buf_a, buf_b, acc, aim, total, steps_ref, starts_ref, span_ref,
):
    sources = (before_ref, middle_ref, after_ref)
    cells = planes - 2
    columns = [(k, c) for k in range(3) for c in range(3)]
    lane = lax.broadcasted_iota(jnp.int32, (16, LANES), 1)
    lift = lax.broadcasted_iota(jnp.int32, (16, LANES), 0)
    mm = functools.partial(jnp.dot, preferred_element_type=jnp.float32)
    for ref in (raw, feat, cols, acc, aim, total, line):
        ref[...] = jnp.zeros_like(ref)

    def append(ref, first, second, at, offset):
        rows = first.shape[0]
        low = jnp.bitwise_and(at, LANES - 1)
        base = lax.shift_right_logical(at, 7) + offset
        first = pltpu.roll(first, low, 1)
        second = pltpu.roll(second, low, 1)
        keep = lane[0:rows] >= low
        place = pl.multiple_of(base * 16, 16)
        ref[pl.ds(place, rows), :] = jnp.where(keep, first, ref[pl.ds(place, rows), :])
        ref[pl.ds(place + 16, rows), :] = jnp.where(keep, second, first)
        ref[pl.ds(place + 32, rows), :] = jnp.where(keep, 0.0, second)

    goal = jnp.int32(0)
    for j in range(planes):
        at = jnp.int32(0)
        for k, c in columns:
            row = ROWS * (c * planes + j)
            first = sources[k][row: row + ROWS, 0:LANES]
            second = sources[k][row: row + ROWS, LANES:]
            count = first[ROWS - 1: ROWS, 0:1].astype(jnp.int32)[0, 0]
            if k == 1 and c == 1 and 0 < j < planes - 1:
                shift = jnp.where(lift[0:8] == 0, j - 0.5, -0.5)
                mark = lift[0:8] < 3
                starts_ref[j - 1] = goal
                append(
                    aim,
                    jnp.where(mark, first[0:8] + shift, float(j)),
                    jnp.where(mark, second[0:8] + shift, float(j)),
                    goal,
                    0,
                )
                goal = goal + count
            shift = (
                jnp.where(lift < 3, -0.5, 0.0)
                + jnp.where(lift == 1, float(c - 1), 0.0)
                + jnp.where(lift == 2, float(k - 1), 0.0)
            )[0:ROWS]
            append(raw, first + shift, second + shift, at, j * BLOCKS)
            at = at + count
        steps_ref[j] = jnp.maximum(lax.shift_right_logical(at + CAP - 1, 8), 1)
    starts_ref[cells] = goal
    for j in range(planes):
        span_ref[j, 0] = lax.shift_right_logical(starts_ref[max(j - 2, 0)], 8)
        span_ref[j, 1] = lax.shift_right_logical(starts_ref[min(j, cells - 1) + 1] + CAP - 1, 8)

    def target(tile):
        at = pl.multiple_of(tile * 32, 32)
        return jnp.concatenate([aim[pl.ds(at, 8), :], aim[pl.ds(at + 16, 8), :]], axis=1)

    def plane_body(j, carry):
        plane = j.astype(jnp.float32)
        steps = steps_ref[j]

        def tile_body(tile, carry):
            spot = target(tile)
            x = [spot[0:1] - plane, spot[1:2], spot[2:3]]
            size = x[0] * x[0] + x[1] * x[1] + x[2] * x[2]
            size = jnp.where(jnp.abs(spot[3:4] - plane) < 1.5, size, 1e30)
            for n in range(3):
                part = [v.astype(jnp.float32) for v in halves(-2.0 * x[n], 3)]
                for r, p in enumerate((0, 1, 0, 1, 2, 0)):
                    line[6 * n + r: 6 * n + r + 1, :] = part[p]
            line[18:21, :] = jnp.ones((3, CAP), jnp.float32)
            for r, p in enumerate(halves(size, 3)):
                line[21 + r: 22 + r, :] = p.astype(jnp.float32)
            right_d[j * TILES + tile] = line[...].astype(jnp.bfloat16)
            return carry

        lax.fori_loop(span_ref[j, 0], span_ref[j, 1], tile_body, 0)

        def group_body(g, carry):
            start = pl.multiple_of((j * BLOCKS + g * 8) * 16, 128)
            row = [raw[pl.ds(start + r, 8, stride=16), :] for r in range(9)]
            y = row[0:3]
            rows3, rows5 = features(y, row[3:6], row[6:9])
            for r, value in rows3.items():
                feat[pl.ds(r, 8, stride=NUM3 + NUM5), :] = value
            for r, value in rows5.items():
                feat[pl.ds(NUM3 + r, 8, stride=NUM3 + NUM5), :] = value
            for n in range(3):
                part = [v.astype(jnp.float32) for v in halves(y[n], 3)]
                for r, p in enumerate((0, 0, 1, 1, 0, 2)):
                    cols[pl.ds(6 * n + r, 8, stride=32), :] = part[p]
            size = y[0] * y[0] + y[1] * y[1] + (y[2] * y[2] + CORE_SQUARE)
            for r, p in enumerate(halves(size, 3)):
                cols[pl.ds(18 + r, 8, stride=32), :] = p.astype(jnp.float32)
            for r in range(3):
                cols[pl.ds(21 + r, 8, stride=32), :] = jnp.ones((8, LANES), jnp.float32)

            def chunk_body(c, carry):
                index = j * CHUNKS + c
                for h in range(2):
                    q = (c - g * 4) * 2 + h
                    span = slice(h * LANES, (h + 1) * LANES)
                    at = pl.multiple_of(q * (NUM3 + NUM5), 16)
                    piece = halves(feat[pl.ds(at, NUM3), :], 3)
                    for n in range(3):
                        left3[index, n * NUM3: (n + 1) * NUM3, span] = piece[n]
                    piece = halves(feat[pl.ds(at + NUM3, NUM5), :], 3)
                    for n in range(3):
                        left5[index, n * NUM5: (n + 1) * NUM5, span] = piece[n]
                    turned = jnp.transpose(cols[pl.ds(pl.multiple_of(q * 32, 32), 32), :])
                    left_d[index, span, :] = turned.astype(jnp.bfloat16)
                return carry

            lax.fori_loop(g * 4, jnp.minimum(g * 4 + 4, steps), chunk_body, 0)
            return carry

        lax.fori_loop(0, lax.shift_right_logical(steps + 3, 2), group_body, 0)
        return carry

    lax.fori_loop(0, planes, plane_body, 0)

    def advance(item):
        j, tile, c = item
        wrap = c + 1 >= steps_ref[j]
        turn = wrap & (tile + 1 >= span_ref[j, 1])
        end = turn & (j + 1 >= planes)
        later = jnp.minimum(j + 1, planes - 1)
        new_j = jnp.where(turn, later, j)
        new_tile = jnp.where(turn, span_ref[later, 0], jnp.where(wrap, tile + 1, tile))
        new_c = jnp.where(wrap, 0, c + 1)
        return (new_j, jnp.where(end, tile, new_tile), jnp.where(end, c, new_c))

    def weigh(item, buf):
        j, tile, c = item
        apart = mm(left_d[j * CHUNKS + c], right_d[j * TILES + tile])
        for s in range(CAP // 16):
            span = slice(s * 16, (s + 1) * 16)
            inv = lax.rsqrt(apart[span, :])
            square = inv * inv
            cube = square * inv
            fifth = cube * square
            buf[0, span, :], buf[1, span, :] = halves(cube, 2)
            buf[2, span, :], buf[3, span, :] = halves(fifth, 2)

    def gather(item, buf, live):
        j, tile, c = item
        index = j * CHUNKS + c
        slot = jnp.where(live, j * TILES + tile, planes * TILES)
        a = mm(left3[index], buf[0])
        b = mm(left3[index, 0:2 * NUM3, :], buf[1])
        acc[slot, 0:NUM3, :] += (
            a[0:NUM3] + (a[NUM3:2 * NUM3] + b[0:NUM3]) + (a[2 * NUM3:] + b[NUM3:])
        )
        a = mm(left5[index], buf[2])
        b = mm(left5[index, 0:2 * NUM5, :], buf[3])
        acc[slot, NUM3:, :] += (
            a[0:NUM5] + (a[NUM5:2 * NUM5] + b[0:NUM5]) + (a[2 * NUM5:] + b[NUM5:])
        )

    count = jnp.int32(0)
    for j in range(planes):
        count = count + steps_ref[j] * (span_ref[j, 1] - span_ref[j, 0])

    def work(m, item):
        after = advance(item)
        weigh(after, buf_b)
        gather(item, buf_a, True)
        later = advance(after)
        weigh(later, buf_a)
        gather(after, buf_b, 2 * m + 1 < count)
        return later

    first = (jnp.int32(0), span_ref[0, 0], jnp.int32(0))
    weigh(first, buf_a)
    lax.fori_loop(0, lax.shift_right_logical(count + 1, 1), work, first)

    def finish_plane(j, carry):
        plane = j.astype(jnp.float32)

        def finish(tile, carry):
            spot = target(tile)
            x = [spot[0:1] - plane, spot[1:2], spot[2:3]]
            slot = j * TILES + tile
            both = acc[slot, 0:NUM3, :] + acc[slot, NUM3:2 * NUM3, :]
            linear = both[24:32] + x[0] * both[0:8] + x[1] * both[8:16] + x[2] * both[16:24]
            second = acc[slot, 2 * NUM3:, :]
            v = [
                x[0] * second[n: n + 1] + x[1] * second[3 + n: 4 + n] + x[2] * second[6 + n: 7 + n]
                for n in range(3)
            ]
            scale = 0.5 * (
                second[0:1] + second[4:5] + second[8:9]
                + x[0] * second[9:10] + x[1] * second[10:11] + x[2] * second[11:12]
            )
            v = [v[n] + scale * x[n] for n in range(3)]
            bend = jnp.concatenate(
                [x[a] * v[b] + x[b] * v[a] for a, b in PAIRS] + [jnp.zeros((2, CAP), jnp.float32)],
                axis=0,
            )
            value = linear + bend
            at = pl.multiple_of(tile * 16, 16)
            total[pl.ds(at, 8), :] += value[:, 0:LANES]
            total[pl.ds(at + 8, 8), :] += value[:, LANES:]
            return carry

        lax.fori_loop(span_ref[j, 0], span_ref[j, 1], finish, 0)
        return carry

    lax.fori_loop(0, planes, finish_plane, 0)

    for i in range(cells):
        at = starts_ref[i]
        low = jnp.bitwise_and(at, LANES - 1)
        back = jnp.bitwise_and(LANES - low, LANES - 1)
        place = pl.multiple_of(lax.shift_right_logical(at, 7) * 8, 8)
        part = [pltpu.roll(total[pl.ds(place + 8 * n, 8), :], back, 1) for n in range(3)]
        keep = lane[0:8] < LANES - low
        out_ref[i, :, 0:LANES] = jnp.where(keep, part[0], part[1])
        out_ref[i, :, LANES:] = jnp.where(keep, part[1], part[2])


def near_call(before, sheet, after):
    planes = sheet.shape[0] // (3 * ROWS)
    cells = planes - 2
    vmem = pl.BlockSpec(memory_space=pltpu.VMEM)
    return pl.pallas_call(
        functools.partial(near_kernel, planes),
        out_shape=jax.ShapeDtypeStruct((cells, 8, CAP), jnp.float32),
        in_specs=[vmem, vmem, vmem],
        out_specs=vmem,
        scratch_shapes=[
            pltpu.VMEM((planes * BLOCKS * 16, LANES), jnp.float32),
            pltpu.VMEM((8 * (NUM3 + NUM5), LANES), jnp.float32),
            pltpu.VMEM((8 * 32, LANES), jnp.float32),
            pltpu.VMEM((planes * CHUNKS, 3 * NUM3, CAP), jnp.bfloat16),
            pltpu.VMEM((planes * CHUNKS, 3 * NUM5, CAP), jnp.bfloat16),
            pltpu.VMEM((planes * CHUNKS, CAP, 32), jnp.bfloat16),
            pltpu.VMEM((planes * TILES, 32, CAP), jnp.bfloat16),
            pltpu.VMEM((32, CAP), jnp.float32),
            pltpu.VMEM((4, CAP, CAP), jnp.bfloat16),
            pltpu.VMEM((4, CAP, CAP), jnp.bfloat16),
            pltpu.VMEM((planes * TILES + 1, NUM3 + NUM5, CAP), jnp.float32),
            pltpu.VMEM((10 * 16, LANES), jnp.float32),
            pltpu.VMEM((10 * 8, LANES), jnp.float32),
            pltpu.SMEM((planes,), jnp.int32),
            pltpu.SMEM((cells + 1,), jnp.int32),
            pltpu.SMEM((planes, 2), jnp.int32),
        ],
        compiler_params=pltpu.CompilerParams(vmem_limit_bytes=40 * 1024 * 1024),
        cost_estimate=pl.CostEstimate(flops=10**9, bytes_accessed=10**7, transcendentals=0),
        name="near",
    )(before, sheet, after)


def far_kernel(planes, spans, place_ref, moment_ref, applied_ref, sheet_ref, total, out_ref):
    cells = planes - 2
    span_x, span_y, span_z = spans
    shape = (span_z, LANES)
    half = LANES // 2
    column = lax.broadcasted_iota(jnp.int32, shape, 1)
    moment = []
    for m in range(9):
        value = moment_ref[:, 0, m // 2 * LANES: (m // 2 + 1) * LANES]
        if m % 2:
            value = pltpu.roll(value, half, 1)
        moment.append(jnp.where(column < half, value, 0.0))
    device = column // cells
    source = (
        (device // span_y * cells + column % cells).astype(jnp.float32),
        (device % span_y).astype(jnp.float32),
        lax.broadcasted_iota(jnp.int32, shape, 0).astype(jnp.float32),
    )
    w = (moment[5] - moment[7], moment[6] - moment[2], moment[1] - moment[3])
    index = {}
    for n, (a, b) in enumerate(PAIRS):
        index[a, b] = index[b, a] = n
    for i in range(cells):
        mine = (place_ref[0] * cells + i, place_ref[1], place_ref[2])
        r = [mine[n].astype(jnp.float32) - source[n] for n in range(3)]
        reach = jnp.maximum(jnp.maximum(jnp.abs(r[0]), jnp.abs(r[1])), jnp.abs(r[2]))
        inv = lax.rsqrt(r[0] * r[0] + r[1] * r[1] + r[2] * r[2] + CORE_SQUARE)
        inv = jnp.where(reach > 1.5, inv, 0.0)
        cube = inv * inv * inv
        fifth = cube * inv * inv
        radial = 2.0 * cube + KAPPA * fifth
        along = w[0] * r[0] + w[1] * r[1] + w[2] * r[2]
        turn = [cross(r, (moment[n], moment[3 + n], moment[6 + n])) for n in range(3)]
        slope = (3.0 * SECOND) * along * fifth
        cut = SECOND * cube
        bulk = SECOND * along * (radial - cube)
        front = -FIRST * radial
        stress = []
        for n, (a, b) in enumerate(PAIRS):
            element = (
                front * (turn[b][a] + turn[a][b])
                + slope * r[a] * r[b]
                - cut * (w[a] * r[b] + w[b] * r[a])
            )
            if a == b:
                element = element + bulk
            stress.append(
                jnp.sum(element, axis=(0, 1), keepdims=True)
                + 0.5 * (applied_ref[a, b] + applied_ref[b, a])
                + total[i, n: n + 1, :]
            )
        row = ROWS * (planes + 1 + i)
        t = [sheet_ref[row + 3 + n: row + 4 + n, :] for n in range(3)]
        b = [sheet_ref[row + 6 + n: row + 7 + n, :] for n in range(3)]
        force = [plus([stress[index[m, n]] * b[n] for n in range(3)]) for m in range(3)]
        for n, value in enumerate(cross(force, t)):
            out_ref[n, i, 0, :, :] = value


def pack_kernel(counts_ref, offset_ref, vector_ref, burgers_ref, all_ref, hold, sems):
    cells = offset_ref.shape[1]
    copies = [
        pltpu.make_async_copy(ref, hold.at[n], sems.at[n])
        for n, ref in enumerate((offset_ref, vector_ref, burgers_ref))
    ]
    for copy in copies:
        copy.start()
    slot = lax.broadcasted_iota(jnp.int32, (cells, CAP), 1)
    cell = lax.broadcasted_iota(jnp.int32, (cells, CAP), 0)
    live = jnp.zeros((cells, CAP), jnp.int32)
    for i in range(cells):
        live = jnp.where(cell == i, counts_ref[i], live)
    filled = slot < live
    for copy in copies:
        copy.wait()
    flat = [hold[n].reshape(3, cells, CAP) for n in range(3)]
    offset = [flat[0][n] for n in range(3)]
    tangent = [jnp.where(filled, flat[1][n], 0.0) for n in range(3)]
    charge = [jnp.where(filled, flat[2][n], 0.0) for n in range(3)]
    level = live.astype(jnp.float32)
    for m in range(3):
        for k in range(3):
            value = jnp.sum(charge[m] * tangent[k], axis=1, keepdims=True)
            level = jnp.where(slot == LANES + 3 * m + k, value, level)
    rows = offset + tangent + charge + [level]
    packed = jnp.concatenate([v[i: i + 1] for i in range(cells) for v in rows], axis=0)
    for d in range(all_ref.shape[0]):
        all_ref[d] = packed


def pick_kernel(planes, spans, place_ref, all_ref, sheet_ref, moment_ref):
    span_x, span_y, span_z = spans
    cells = planes - 2
    for dy in range(3):
        y = place_ref[1] + (dy - 1)
        for j in range(planes):
            step = (j + cells - 1) // cells - 1
            c = (j - 1) % cells
            x = place_ref[0] + step
            inside = (x >= 0) & (x < span_x) & (y >= 0) & (y < span_y)
            device = jnp.clip(x, 0, span_x - 1) * span_y + jnp.clip(y, 0, span_y - 1)
            row = ROWS * (dy * planes + j)
            sheet_ref[row: row + ROWS, :] = jnp.where(
                inside, all_ref[device, ROWS * c: ROWS * c + ROWS, :], 0.0
            )
    rows = [
        all_ref[d, ROWS * c + ROWS - 1: ROWS * c + ROWS, LANES:]
        for d in range(span_x * span_y)
        for c in range(cells)
    ]
    rows.append(jnp.zeros((LANES - len(rows), LANES), jnp.float32))
    flip = jnp.transpose(jnp.concatenate(rows, axis=0))
    half = LANES // 2
    line = [
        flip[2 * r: 2 * r + 1] + pltpu.roll(flip[2 * r + 1: 2 * r + 2], half, 1) for r in range(5)
    ]
    line = jnp.concatenate(line, axis=1)
    moment_ref[...] = jnp.broadcast_to(line[None], moment_ref.shape)


def beside(first, last, axis):
    devices = lax.axis_size(axis)
    up = [(i, i + 1) for i in range(devices - 1)]
    down = [(i + 1, i) for i in range(devices - 1)]
    return lax.ppermute(last, axis, up), lax.ppermute(first, axis, down)


def local(seg_offset, seg_vector, burgers, cell_counts, applied):
    cells = seg_offset.shape[1]
    planes = cells + 2
    spans = tuple(lax.axis_size(a) for a in ("gx", "gy", "gz"))
    place = jnp.stack([lax.axis_index(a) for a in ("gx", "gy", "gz")]).astype(jnp.int32)
    devices = spans[0] * spans[1]
    vmem = pl.BlockSpec(memory_space=pltpu.VMEM)
    smem = pl.BlockSpec(memory_space=pltpu.SMEM)
    anywhere = pl.BlockSpec(memory_space=pl.ANY)
    limit = pltpu.CompilerParams(vmem_limit_bytes=40 * 1024 * 1024)
    packed = pl.pallas_call(
        pack_kernel,
        out_shape=jax.ShapeDtypeStruct((devices, cells * ROWS, CAP), jnp.float32),
        in_specs=[smem] + [anywhere] * 3,
        out_specs=vmem,
        scratch_shapes=[
            pltpu.VMEM((3,) + seg_offset.shape, jnp.float32),
            pltpu.SemaphoreType.DMA((3,)),
        ],
        compiler_params=pltpu.CompilerParams(vmem_limit_bytes=60 * 1024 * 1024),
        name="pack",
    )(cell_counts.reshape(cells), seg_offset, seg_vector, burgers)
    every = lax.all_to_all(packed, ("gx", "gy"), 0, 0)
    sheet, moments = pl.pallas_call(
        functools.partial(pick_kernel, planes, spans),
        out_shape=(
            jax.ShapeDtypeStruct((3 * planes * ROWS, CAP), jnp.float32),
            jax.ShapeDtypeStruct((spans[2], 1, 5 * LANES), jnp.float32),
        ),
        in_specs=[smem, vmem],
        out_specs=(vmem, vmem),
        compiler_params=limit,
        name="pick",
    )(place, every)
    before, after = beside(sheet, sheet, "gz")
    moments = lax.all_to_all(moments, "gz", 0, 0)
    total = near_call(before, sheet, after)
    return pl.pallas_call(
        functools.partial(far_kernel, planes, spans),
        out_shape=jax.ShapeDtypeStruct(seg_offset.shape, jnp.float32),
        in_specs=[smem, vmem, smem, vmem, vmem],
        out_specs=vmem,
        compiler_params=limit,
        name="far",
    )(place, moments, applied, sheet, total)


def solution(mesh):
    placed = P(None, "gx", "gy", "gz", None)
    return jax.shard_map(
        local,
        mesh=mesh,
        in_specs=(placed, placed, placed, P("gx", "gy", "gz"), P()),
        out_specs=placed,
        check_vma=False,
    )
```

time: 77.4 us -> 69.3 us (0.90)
  the two profiles are of different devices: /device:TPU:435 before, /device:TPU:35 now
where the time goes in v3:
time: 69.3 us; the launch traced here: 68.9 us
  starting transfers between devices  29.6 us (43%)
  Pallas kernels  25.3 us (37%)
  waiting for transfers between devices  13.8 us (20%)
    pallas_call x1, Pallas kernels, near_call(): pl.pallas_call(functools.partial(near_kernel, planes), out_shape=jax.Shap...  20 us
    all_to_all x1, starting transfers between devices, local(): moments = lax.all_to_all(moments, 'gz', 0, 0)  17.1 us
    all_to_all x1, waiting for transfers between devices, local(): every = lax.all_to_all(packed, ('gx', 'gy'), 0, 0)  10.6 us
    all_to_all x1, starting transfers between devices, local(): every = lax.all_to_all(packed, ('gx', 'gy'), 0, 0)  6.93 us
    ppermute x2, starting transfers between devices, beside(): return (lax.ppermute(last, axis, up), lax.ppermute(first, axis, down))  5.56 us
    ppermute x2, waiting for transfers between devices, beside(): return (lax.ppermute(last, axis, up), lax.ppermute(first, axis, down))  3.21 us
    pallas_call x1, Pallas kernels, local(): pl.pallas_call(pack_kernel, out_shape=jax.ShapeDtypeStruct((devices, cell...  2.38 us
    pallas_call x1, Pallas kernels, local(): pl.pallas_call(functools.partial(far_kernel, planes, spans), out_shape=ja...  1.59 us
  transfers between devices with their start and end apart: 4, of which 2 were waited for; matrix products, arithmetic and copies ran while one was open for 0% of the time, Pallas kernels for 29%

profile of v3, /device:TPU:35, one launch (start us, length us, event | category | flops | bytes accessed | tf_op | source)
XLA Modules:
  0.0 68.9 jit_solution(4590755637415377281)
XLA Ops:
  0.0 2.4 %pack.1 = f32[16,40,256]{2,1,0:T(8,128)} custom-call(s32[4]{0:T(128)} %bitcast.4, f32[3,4,1,1,256]{4,3,2,1,0:T(1,128)} %offset_ref.1, f32[3,4,1,1,256]{4,3,2,1,0:T(1,128)} %vector_ref.1, f32[3,4,1,1,256]{4,3,2,1,0:T(1,128)} %burgers_ref.1), custom_call_target="tpu_custom_call" | custom-call | tf_op jit(solution)/shard_map/pack/pallas_call | solution.py:503
  2.4 6.9 %all-to-all-start = ((f32[16,40,256]{2,1,0:T(8,128)}), f32[16,40,256]{2,1,0:T(8,128)S(1)}, u32[]{:S(2)}, u32[]{:S(2)}) async-start(f32[16,40,256]{2,1,0:T(8,128)} %pack.1), calls=%async_computation | async-start | bytes 1310720 | tf_op jit(solution)/shard_map/all_to_all | solution.py:515
  9.3 0.1 pad_add_fusion.place_ref
  9.4 10.6 %all-to-all-done.all_ref = f32[16,40,256]{2,1,0:T(8,128)S(1)} async-done(((f32[16,40,256]{2,1,0:T(8,128)}), f32[16,40,256]{2,1,0:T(8,128)S(1)}, u32[]{:S(2)}, u32[]{:S(2)}) %all-to-all-start) | async-done | bytes 655392 | tf_op jit(solution)/shard_map/all_to_all | solution.py:515
  20.0 1.3 %pick.1 = (f32[180,256]{1,0:T(8,128)S(1)}, f32[32,1,640]{2,1,0:T(1,128)}) custom-call(s32[3]{0:T(128)S(1)} %pad_add_fusion.place_ref, f32[16,40,256]{2,1,0:T(8,128)S(1)} %all-to-all-done.all_ref), custom_call_target="tpu_custom_call" | custom-call | tf_op jit(solution)/shard_map/pick/pallas_call | solution.py:516
  21.4 17.1 %all-to-all-start.1 = ((f32[32,1,640]{2,1,0:T(1,128)}), f32[32,1,640]{2,1,0:T(1,128)S(1)}, u32[]{:S(2)}, u32[]{:S(2)}) async-start(f32[32,1,640]{2,1,0:T(1,128)} %get-tuple-element.7), calls=%async_computation.1 | async-start | bytes 163840 | tf_op jit(solution)/shard_map/all_to_all | solution.py:528
  38.5 0.0 copy-start
  38.5 2.3 %collective-permute-start.1 = (f32[180,256]{1,0:T(8,128)S(1)}, f32[180,256]{1,0:T(8,128)S(1)}, u32[]{:S(2)}, u32[]{:S(2)}) collective-permute-start(f32[180,256]{1,0:T(8,128)S(1)} %get-tuple-element.8.middle_ref.sheet_ref), channel_id=1, source_target_pairs={{1,0},{2,1},{3,2},{4,3},{5,4},{6,5},{7,6},{8,7},{9,8},{10,9},{11,1... | collective-permute-start | bytes 552968 | tf_op jit(solution)/shard_map/ppermute | solution.py:490
  40.8 3.3 %collective-permute-start = (f32[180,256]{1,0:T(8,128)S(1)}, f32[180,256]{1,0:T(8,128)S(1)}, u32[]{:S(2)}, u32[]{:S(2)}) collective-permute-start(f32[180,256]{1,0:T(8,128)S(1)} %get-tuple-element.8.middle_ref.sheet_ref), channel_id=1, source_target_pairs={{0,1},{1,2},{2,3},{3,4},{4,5},{5,6},{6,7},{7,8},{8,9},{9,10},{10,1... | collective-permute-start | bytes 552968 | tf_op jit(solution)/shard_map/ppermute | solution.py:490
  44.1 3.2 %collective-permute-done.1.after_ref = f32[180,256]{1,0:T(8,128)S(1)} collective-permute-done((f32[180,256]{1,0:T(8,128)S(1)}, f32[180,256]{1,0:T(8,128)S(1)}, u32[]{:S(2)}, u32[]{:S(2)}) %collective-permute-start.1) | collective-permute-done | bytes 184352 | tf_op jit(solution)/shard_map/ppermute | solution.py:490
  47.3 0.0 collective-permute-done.before_ref
  47.3 20.0 %near.1.total = f32[4,8,256]{2,1,0:T(8,128)S(1)} custom-call(f32[180,256]{1,0:T(8,128)S(1)} %collective-permute-done.before_ref, f32[180,256]{1,0:T(8,128)S(1)} %get-tuple-element.8.middle_ref.sheet_ref, f32[180,256]{1,0:T(8,128)S(1)} %collective-permute-done.1.after_ref), custom_call_target="tpu_custom_call" | custom-call | flops 1000000000 | bytes 10000000 | tf_op jit(solution)/shard_map/near/pallas_call | solution.py:337
  67.3 0.0 all-to-all-done.1.moment_ref
  67.3 0.0 copy-done
  67.3 1.6 %far.1 = f32[3,4,1,1,256]{4,3,2,1,0:T(1,128)} custom-call(s32[3]{0:T(128)S(1)} %pad_add_fusion.place_ref, f32[32,1,640]{2,1,0:T(1,128)S(1)} %all-to-all-done.1.moment_ref, f32[3,3]{1,0:T(4,128)S(1)} %copy-done, f32[180,256]{1,0:T(8,128)S(1)} %get-tuple-element.8.middle_ref.sheet_ref, f32[4,8,256]{2,1,0:T(8,128)S(1)} %near.1.total), custom_call_target="tpu_custom_call" | custom-call | tf_op jit(solution)/shard_map/far/pallas_call | solution.py:530
Async XLA Ops:
  2.4 17.6 %all-to-all-start = ((f32[16,40,256]{2,1,0:T(8,128)}), f32[16,40,256]{2,1,0:T(8,128)S(1)}, u32[]{:S(2)}, u32[]{:S(2)}) async-start(f32[16,40,256]{2,1,0:T(8,128)} %pack.1), calls=%async_computation | async-start | bytes 1310720 | tf_op jit(solution)/shard_map/all_to_all | solution.py:515
  21.4 46.0 %all-to-all-start.1 = ((f32[32,1,640]{2,1,0:T(1,128)}), f32[32,1,640]{2,1,0:T(1,128)S(1)}, u32[]{:S(2)}, u32[]{:S(2)}) async-start(f32[32,1,640]{2,1,0:T(1,128)} %get-tuple-element.7), calls=%async_computation.1 | async-start | bytes 163840 | tf_op jit(solution)/shard_map/all_to_all | solution.py:528
  38.5 28.9 %copy-start = (f32[3,3]{1,0:T(4,128)S(1)}, f32[3,3]{1,0:T(4,128)}, u32[]{:S(2)}) copy-start(f32[3,3]{1,0:T(4,128)} %applied_ref.1) | copy-start | bytes 112
  38.5 8.8 %collective-permute-start.1 = (f32[180,256]{1,0:T(8,128)S(1)}, f32[180,256]{1,0:T(8,128)S(1)}, u32[]{:S(2)}, u32[]{:S(2)}) collective-permute-start(f32[180,256]{1,0:T(8,128)S(1)} %get-tuple-element.8.middle_ref.sheet_ref), channel_id=1, source_target_pairs={{1,0},{2,1},{3,2},{4,3},{5,4},{6,5},{7,6},{8,7},{9,8},{10,9},{11,1... | collective-permute-start | bytes 552968 | tf_op jit(solution)/shard_map/ppermute | solution.py:490
  40.8 6.5 %collective-permute-start = (f32[180,256]{1,0:T(8,128)S(1)}, f32[180,256]{1,0:T(8,128)S(1)}, u32[]{:S(2)}, u32[]{:S(2)}) collective-permute-start(f32[180,256]{1,0:T(8,128)S(1)} %get-tuple-element.8.middle_ref.sheet_ref), channel_id=1, source_target_pairs={{0,1},{1,2},{2,3},{3,4},{4,5},{5,6},{6,7},{7,8},{8,9},{9,10},{10,1... | collective-permute-start | bytes 552968 | tf_op jit(solution)/shard_map/ppermute | solution.py:490

commit v4 on v3

--- a/solution.py
+++ b/solution.py
@@ -16,11 +16,12 @@
 LANES = 128
 ROWS = 10
 PAIRS = ((0, 0), (0, 1), (0, 2), (1, 1), (1, 2), (2, 2))
-NUM3 = 32
-NUM5 = 48
+NUM3 = 24
+NUM5 = 40
+NUM = NUM3 + NUM5
 BLOCKS = 24
-CHUNKS = 9
-TILES = 4
+CHUNKS = 10
+TILES = 3
 
 
 def cross(a, b):
@@ -72,7 +73,7 @@
         zero3, zero5 = [], [doty[i] * y[j]]
         for m in range(3):
             if lin3[m, n] is not None:
-                rows3[8 * m + n] = lin3[m, n]
+                rows3[6 * m + n] = lin3[m, n]
                 zero3.append(lin3[m, n] * y[m])
             quad = [wy[m][i] * y[j]]
             if m == i:
@@ -82,14 +83,14 @@
             if lin5[m, n] is not None:
                 quad.append(lin5[m, n])
                 zero5.append(lin5[m, n] * y[m])
-            rows5[8 * m + n] = plus(quad)
+            rows5[6 * m + n] = plus(quad)
         if zero3:
-            rows3[24 + n] = -plus(zero3)
-        rows5[24 + n] = -plus(zero5)
+            rows3[18 + n] = -plus(zero3)
+        rows5[18 + n] = -plus(zero5)
     for m in range(3):
         for n in range(3):
-            rows5[32 + 3 * m + n] = -wy[m][n]
-        rows5[41 + m] = w3[m]
+            rows5[24 + 3 * m + n] = -wy[m][n]
+        rows5[33 + m] = w3[m]
     return rows3, rows5
 
 
@@ -105,8 +106,7 @@
 
 def near_kernel(
     planes, before_ref, middle_ref, after_ref, out_ref,
-    raw, feat, cols, left3, left5, left_d, right_d, line,
-    buf_a, buf_b, acc, aim, total, steps_ref, starts_ref, span_ref,
+    raw, feat, cols, left3, left5, left_d, right_d, spots, line, buf_a, buf_b, acc, aim, total, steps_ref, starts_ref, tiles_ref,
 ):
     sources = (before_ref, middle_ref, after_ref)
     cells = planes - 2
@@ -114,7 +114,7 @@
     lane = lax.broadcasted_iota(jnp.int32, (16, LANES), 1)
     lift = lax.broadcasted_iota(jnp.int32, (16, LANES), 0)
     mm = functools.partial(jnp.dot, preferred_element_type=jnp.float32)
-    for ref in (raw, feat, cols, acc, aim, total, line):
+    for ref in (raw, aim, total, line):
         ref[...] = jnp.zeros_like(ref)
 
     def append(ref, first, second, at, offset):
@@ -159,85 +159,106 @@
         steps_ref[j] = jnp.maximum(lax.shift_right_logical(at + CAP - 1, 8), 1)
     starts_ref[cells] = goal
     for j in range(planes):
-        span_ref[j, 0] = lax.shift_right_logical(starts_ref[max(j - 2, 0)], 8)
-        span_ref[j, 1] = lax.shift_right_logical(starts_ref[min(j, cells - 1) + 1] + CAP - 1, 8)
-
-    def target(tile):
-        at = pl.multiple_of(tile * 32, 32)
-        return jnp.concatenate([aim[pl.ds(at, 8), :], aim[pl.ds(at + 16, 8), :]], axis=1)
-
-    def plane_body(j, carry):
-        plane = j.astype(jnp.float32)
-        steps = steps_ref[j]
-
-        def tile_body(tile, carry):
-            spot = target(tile)
-            x = [spot[0:1] - plane, spot[1:2], spot[2:3]]
+        reach = starts_ref[min(j, cells - 1) + 1] - starts_ref[max(j - 2, 0)]
+        tiles_ref[j] = lax.shift_right_logical(reach + CAP - 1, 8)
+
+    for j in range(planes):
+        for tile in range(min(j, cells - 1) + 1 - max(j - 2, 0)):
+            at = starts_ref[max(j - 2, 0)] + CAP * tile
+            at = jnp.minimum(at, starts_ref[cells])
+            low = jnp.bitwise_and(at, LANES - 1)
+            back = jnp.bitwise_and(LANES - low, LANES - 1)
+            place = pl.multiple_of(lax.shift_right_logical(at, 7) * 16, 16)
+            part = [pltpu.roll(aim[pl.ds(place + 16 * n, 8), :], back, 1) for n in range(3)]
+            keep = lane[0:8] < LANES - low
+            spot = jnp.concatenate(
+                [jnp.where(keep, part[0], part[1]), jnp.where(keep, part[1], part[2])], axis=1
+            )
+            x = [spot[0:1] - float(j), spot[1:2], spot[2:3]]
             size = x[0] * x[0] + x[1] * x[1] + x[2] * x[2]
-            size = jnp.where(jnp.abs(spot[3:4] - plane) < 1.5, size, 1e30)
+            size = jnp.where(jnp.abs(spot[3:4] - float(j)) < 1.5, size, 1e30)
+            slot = j * TILES + tile
             for n in range(3):
+                spots[slot, n: n + 1, :] = x[n]
                 part = [v.astype(jnp.float32) for v in halves(-2.0 * x[n], 3)]
                 for r, p in enumerate((0, 1, 0, 1, 2, 0)):
-                    line[6 * n + r: 6 * n + r + 1, :] = part[p]
-            line[18:21, :] = jnp.ones((3, CAP), jnp.float32)
+                    line[slot, 6 * n + r: 6 * n + r + 1, :] = part[p]
+            line[slot, 18:21, :] = jnp.ones((3, CAP), jnp.float32)
             for r, p in enumerate(halves(size, 3)):
-                line[21 + r: 22 + r, :] = p.astype(jnp.float32)
-            right_d[j * TILES + tile] = line[...].astype(jnp.bfloat16)
-            return carry
-
-        lax.fori_loop(span_ref[j, 0], span_ref[j, 1], tile_body, 0)
-
-        def group_body(g, carry):
-            start = pl.multiple_of((j * BLOCKS + g * 8) * 16, 128)
-            row = [raw[pl.ds(start + r, 8, stride=16), :] for r in range(9)]
-            y = row[0:3]
-            rows3, rows5 = features(y, row[3:6], row[6:9])
-            for r, value in rows3.items():
-                feat[pl.ds(r, 8, stride=NUM3 + NUM5), :] = value
-            for r, value in rows5.items():
-                feat[pl.ds(NUM3 + r, 8, stride=NUM3 + NUM5), :] = value
-            for n in range(3):
-                part = [v.astype(jnp.float32) for v in halves(y[n], 3)]
-                for r, p in enumerate((0, 0, 1, 1, 0, 2)):
-                    cols[pl.ds(6 * n + r, 8, stride=32), :] = part[p]
-            size = y[0] * y[0] + y[1] * y[1] + (y[2] * y[2] + CORE_SQUARE)
-            for r, p in enumerate(halves(size, 3)):
-                cols[pl.ds(18 + r, 8, stride=32), :] = p.astype(jnp.float32)
-            for r in range(3):
-                cols[pl.ds(21 + r, 8, stride=32), :] = jnp.ones((8, LANES), jnp.float32)
-
-            def chunk_body(c, carry):
-                index = j * CHUNKS + c
-                for h in range(2):
-                    q = (c - g * 4) * 2 + h
-                    span = slice(h * LANES, (h + 1) * LANES)
-                    at = pl.multiple_of(q * (NUM3 + NUM5), 16)
-                    piece = halves(feat[pl.ds(at, NUM3), :], 3)
-                    for n in range(3):
-                        left3[index, n * NUM3: (n + 1) * NUM3, span] = piece[n]
-                    piece = halves(feat[pl.ds(at + NUM3, NUM5), :], 3)
-                    for n in range(3):
-                        left5[index, n * NUM5: (n + 1) * NUM5, span] = piece[n]
-                    turned = jnp.transpose(cols[pl.ds(pl.multiple_of(q * 32, 32), 32), :])
-                    left_d[index, span, :] = turned.astype(jnp.bfloat16)
-                return carry
-
-            lax.fori_loop(g * 4, jnp.minimum(g * 4 + 4, steps), chunk_body, 0)
-            return carry
-
-        lax.fori_loop(0, lax.shift_right_logical(steps + 3, 2), group_body, 0)
-        return carry
-
-    lax.fori_loop(0, planes, plane_body, 0)
+                line[slot, 21 + r: 22 + r, :] = p.astype(jnp.float32)
+            right_d[slot] = line[slot].astype(jnp.bfloat16)
+
+    def describe(j, g):
+        start = (j * BLOCKS + g * 8) * 16
+        row = jnp.swapaxes(jnp.stack([raw[start + 16 * q: start + 16 * q + 8, :] for q in range(8)]), 0, 1)
+        row = [row[r] for r in range(8)] + [raw[pl.ds(start + 8, 8, stride=16), :]]
+        rows3, rows5 = features(row[0:3], row[3:6], row[6:9])
+        base = (j * BLOCKS + g * 8) * NUM
+        def spread(ref, first, step, rows):
+            for k in range(0, len(rows), 8):
+                part = jnp.swapaxes(jnp.stack(rows[k: k + 8]), 0, 1)
+                for q in range(8):
+                    ref[first + q * step + k: first + q * step + k + 8, :] = part[q]
+
+        none = jnp.zeros((8, LANES), jnp.float32)
+        spread(feat, base, NUM, [rows3.get(r, none) for r in range(NUM3)] + [rows5.get(r, none) for r in range(NUM5)])
+        y = row[0:3]
+        size = y[0] * y[0] + y[1] * y[1] + (y[2] * y[2] + CORE_SQUARE)
+        line_rows = []
+        for n in range(3):
+            part = [v.astype(jnp.float32) for v in halves(y[n], 3)]
+            line_rows += [part[p] for p in (0, 0, 1, 1, 0, 2)]
+        line_rows += [p.astype(jnp.float32) for p in halves(size, 3)]
+        line_rows += [none + 1.0] * 3 + [none] * 8
+        spread(cols, (j * BLOCKS + g * 8) * 32, 32, line_rows)
+
+    for j in range(planes):
+        describe(j, 0)
+    for g in range(1, BLOCKS // 8):
+        for j in range(planes):
+            pl.when(steps_ref[j] > 4 * g)(functools.partial(describe, j, g))
+
+    def rest(value):
+        return value - value.astype(jnp.bfloat16).astype(jnp.float32)
+
+    def split_body(n, state):
+        j, c = state
+        for part in range(2):
+            index = j * CHUNKS + c + part
+            for h in range(2):
+                block = j * BLOCKS + 2 * (c + part) + h
+                span = slice(h * LANES, (h + 1) * LANES)
+                at = pl.multiple_of(block * NUM, 8)
+                value = feat[pl.ds(at, NUM3), :]
+                left3[index, :, span] = jnp.concatenate([value, rest(value)], axis=0).astype(
+                    jnp.bfloat16
+                )
+                value = feat[pl.ds(at + NUM3, NUM5), :]
+                second = rest(value)
+                third = rest(second)
+                left5[index, :, span] = jnp.concatenate(
+                    [value, second, third, jnp.zeros((8, LANES), jnp.float32)], axis=0
+                ).astype(jnp.bfloat16)
+                turned = jnp.transpose(cols[pl.ds(pl.multiple_of(block * 32, 32), 32), :])
+                left_d[index, span, :] = turned.astype(jnp.bfloat16)
+        wrap = c + 2 >= steps_ref[j]
+        return (
+            jnp.where(wrap, jnp.minimum(j + 1, planes - 1), j),
+            jnp.where(wrap, 0, c + 2),
+        )
+
+    pieces = jnp.int32(0)
+    for j in range(planes):
+        pieces = pieces + lax.shift_right_logical(steps_ref[j] + 1, 1)
+    lax.fori_loop(0, pieces, split_body, (jnp.int32(0), jnp.int32(0)))
 
     def advance(item):
         j, tile, c = item
         wrap = c + 1 >= steps_ref[j]
-        turn = wrap & (tile + 1 >= span_ref[j, 1])
+        turn = wrap & (tile + 1 >= tiles_ref[j])
         end = turn & (j + 1 >= planes)
-        later = jnp.minimum(j + 1, planes - 1)
-        new_j = jnp.where(turn, later, j)
-        new_tile = jnp.where(turn, span_ref[later, 0], jnp.where(wrap, tile + 1, tile))
+        new_j = jnp.where(turn, jnp.minimum(j + 1, planes - 1), j)
+        new_tile = jnp.where(turn, 0, jnp.where(wrap, tile + 1, tile))
         new_c = jnp.where(wrap, 0, c + 1)
         return (new_j, jnp.where(end, tile, new_tile), jnp.where(end, c, new_c))
 
@@ -258,19 +279,18 @@
         index = j * CHUNKS + c
         slot = jnp.where(live, j * TILES + tile, planes * TILES)
         a = mm(left3[index], buf[0])
-        b = mm(left3[index, 0:2 * NUM3, :], buf[1])
-        acc[slot, 0:NUM3, :] += (
-            a[0:NUM3] + (a[NUM3:2 * NUM3] + b[0:NUM3]) + (a[2 * NUM3:] + b[NUM3:])
-        )
-        a = mm(left5[index], buf[2])
-        b = mm(left5[index, 0:2 * NUM5, :], buf[3])
-        acc[slot, NUM3:, :] += (
-            a[0:NUM5] + (a[NUM5:2 * NUM5] + b[0:NUM5]) + (a[2 * NUM5:] + b[NUM5:])
+        b = mm(left3[index, 0:32, :], buf[1])
+        d = mm(left5[index], buf[2])
+        e = mm(left5[index, 0:2 * NUM5, :], buf[3])
+        old = jnp.where(c == 0, 0.0, acc[slot])
+        acc[slot, 0:NUM3, :] = old[0:NUM3] + (a[0:NUM3] + (a[NUM3:] + b[0:NUM3]))
+        acc[slot, NUM3:, :] = old[NUM3:] + (
+            d[0:NUM5] + (d[NUM5:2 * NUM5] + e[0:NUM5]) + (d[2 * NUM5:3 * NUM5] + e[NUM5:])
         )
 
     count = jnp.int32(0)
     for j in range(planes):
-        count = count + steps_ref[j] * (span_ref[j, 1] - span_ref[j, 0])
+        count = count + steps_ref[j] * tiles_ref[j]
 
     def work(m, item):
         after = advance(item)
@@ -281,19 +301,16 @@
         gather(after, buf_b, 2 * m + 1 < count)
         return later
 
-    first = (jnp.int32(0), span_ref[0, 0], jnp.int32(0))
+    first = (jnp.int32(0), jnp.int32(0), jnp.int32(0))
     weigh(first, buf_a)
     lax.fori_loop(0, lax.shift_right_logical(count + 1, 1), work, first)
 
     def finish_plane(j, carry):
-        plane = j.astype(jnp.float32)
-
         def finish(tile, carry):
-            spot = target(tile)
-            x = [spot[0:1] - plane, spot[1:2], spot[2:3]]
             slot = j * TILES + tile
+            x = [spots[slot, n: n + 1, :] for n in range(3)]
             both = acc[slot, 0:NUM3, :] + acc[slot, NUM3:2 * NUM3, :]
-            linear = both[24:32] + x[0] * both[0:8] + x[1] * both[8:16] + x[2] * both[16:24]
+            linear = both[18:24] + x[0] * both[0:6] + x[1] * both[6:12] + x[2] * both[12:18]
             second = acc[slot, 2 * NUM3:, :]
             v = [
                 x[0] * second[n: n + 1] + x[1] * second[3 + n: 4 + n] + x[2] * second[6 + n: 7 + n]
@@ -304,17 +321,21 @@
                 + x[0] * second[9:10] + x[1] * second[10:11] + x[2] * second[11:12]
             )
             v = [v[n] + scale * x[n] for n in range(3)]
-            bend = jnp.concatenate(
-                [x[a] * v[b] + x[b] * v[a] for a, b in PAIRS] + [jnp.zeros((2, CAP), jnp.float32)],
-                axis=0,
-            )
+            bend = jnp.concatenate([x[a] * v[b] + x[b] * v[a] for a, b in PAIRS], axis=0)
             value = linear + bend
-            at = pl.multiple_of(tile * 16, 16)
-            total[pl.ds(at, 8), :] += value[:, 0:LANES]
-            total[pl.ds(at + 8, 8), :] += value[:, LANES:]
+            value = jnp.concatenate([value, jnp.zeros((2, CAP), jnp.float32)], axis=0)
+            at = starts_ref[jnp.maximum(j - 2, 0)] + CAP * tile
+            low = jnp.bitwise_and(at, LANES - 1)
+            place = pl.multiple_of(lax.shift_right_logical(at, 7) * 8, 8)
+            keep = lane[0:8] >= low
+            one = pltpu.roll(value[:, 0:LANES], low, 1)
+            two = pltpu.roll(value[:, LANES:], low, 1)
+            total[pl.ds(place, 8), :] += jnp.where(keep, one, 0.0)
+            total[pl.ds(place + 8, 8), :] += jnp.where(keep, two, one)
+            total[pl.ds(place + 16, 8), :] += jnp.where(keep, 0.0, two)
             return carry
 
-        lax.fori_loop(span_ref[j, 0], span_ref[j, 1], finish, 0)
+        lax.fori_loop(0, tiles_ref[j], finish, 0)
         return carry
 
     lax.fori_loop(0, planes, finish_plane, 0)
@@ -341,24 +362,25 @@
         out_specs=vmem,
         scratch_shapes=[
             pltpu.VMEM((planes * BLOCKS * 16, LANES), jnp.float32),
-            pltpu.VMEM((8 * (NUM3 + NUM5), LANES), jnp.float32),
-            pltpu.VMEM((8 * 32, LANES), jnp.float32),
-            pltpu.VMEM((planes * CHUNKS, 3 * NUM3, CAP), jnp.bfloat16),
-            pltpu.VMEM((planes * CHUNKS, 3 * NUM5, CAP), jnp.bfloat16),
+            pltpu.VMEM((planes * BLOCKS * NUM, LANES), jnp.float32),
+            pltpu.VMEM((planes * BLOCKS * 32, LANES), jnp.float32),
+            pltpu.VMEM((planes * CHUNKS, 48, CAP), jnp.bfloat16),
+            pltpu.VMEM((planes * CHUNKS, 128, CAP), jnp.bfloat16),
             pltpu.VMEM((planes * CHUNKS, CAP, 32), jnp.bfloat16),
             pltpu.VMEM((planes * TILES, 32, CAP), jnp.bfloat16),
-            pltpu.VMEM((32, CAP), jnp.float32),
+            pltpu.VMEM((planes * TILES, 8, CAP), jnp.float32),
+            pltpu.VMEM((planes * TILES, 32, CAP), jnp.float32),
             pltpu.VMEM((4, CAP, CAP), jnp.bfloat16),
             pltpu.VMEM((4, CAP, CAP), jnp.bfloat16),
-            pltpu.VMEM((planes * TILES + 1, NUM3 + NUM5, CAP), jnp.float32),
+            pltpu.VMEM((planes * TILES + 1, NUM, CAP), jnp.float32),
             pltpu.VMEM((10 * 16, LANES), jnp.float32),
             pltpu.VMEM((10 * 8, LANES), jnp.float32),
             pltpu.SMEM((planes,), jnp.int32),
             pltpu.SMEM((cells + 1,), jnp.int32),
-            pltpu.SMEM((planes, 2), jnp.int32),
+            pltpu.SMEM((planes,), jnp.int32),
         ],
         compiler_params=pltpu.CompilerParams(vmem_limit_bytes=40 * 1024 * 1024),
-        cost_estimate=pl.CostEstimate(flops=10**9, bytes_accessed=10**7, transcendentals=0),
+        cost_estimate=pl.CostEstimate(flops=3 * 10**10, bytes_accessed=10**7, transcendentals=0),
         name="near",
     )(before, sheet, after)
 

time: 69.3 us -> 60.8 us (0.88)
  the two profiles are of different devices: /device:TPU:35 before, /device:TPU:1 now
where the time goes in v4:
time: 60.8 us; the launch traced here: 60.4 us
  starting transfers between devices  31.1 us (51%)
  waiting for transfers between devices  17.8 us (29%)
  Pallas kernels  11.3 us (19%)
    all_to_all x1, starting transfers between devices, local(): moments = lax.all_to_all(moments, 'gz', 0, 0)  14.5 us
    all_to_all x1, waiting for transfers between devices, local(): every = lax.all_to_all(packed, ('gx', 'gy'), 0, 0)  10.2 us
    ppermute x2, starting transfers between devices, beside(): return (lax.ppermute(last, axis, up), lax.ppermute(first, axis, down))  8.99 us
    all_to_all x1, waiting for transfers between devices, local(): moments = lax.all_to_all(moments, 'gz', 0, 0)  7.65 us
    all_to_all x1, starting transfers between devices, local(): every = lax.all_to_all(packed, ('gx', 'gy'), 0, 0)  7.6 us
    pallas_call x1, Pallas kernels, near_call(): pl.pallas_call(functools.partial(near_kernel, planes), out_shape=jax.Shap...  6.02 us
    pallas_call x1, Pallas kernels, local(): pl.pallas_call(pack_kernel, out_shape=jax.ShapeDtypeStruct((devices, cell...  2.38 us
    pallas_call x1, Pallas kernels, local(): pl.pallas_call(functools.partial(far_kernel, planes, spans), out_shape=ja...  1.59 us
  transfers between devices with their start and end apart: 4, of which 2 were waited for; matrix products, arithmetic and copies ran while one was open for 0% of the time, Pallas kernels for 10%

profile of v4, /device:TPU:1, one launch (start us, length us, event | category | flops | bytes accessed | tf_op | source)
XLA Modules:
  0.0 60.4 jit_solution(16886762433254317007)
XLA Ops:
  0.0 2.4 %pack.1 = f32[16,40,256]{2,1,0:T(8,128)} custom-call(s32[4]{0:T(128)} %bitcast.4, f32[3,4,1,1,256]{4,3,2,1,0:T(1,128)} %offset_ref.1, f32[3,4,1,1,256]{4,3,2,1,0:T(1,128)} %vector_ref.1, f32[3,4,1,1,256]{4,3,2,1,0:T(1,128)} %burgers_ref.1), custom_call_target="tpu_custom_call" | custom-call | tf_op jit(solution)/shard_map/pack/pallas_call | solution.py:525
  2.4 7.6 %all-to-all-start = ((f32[16,40,256]{2,1,0:T(8,128)}), f32[16,40,256]{2,1,0:T(8,128)S(1)}, u32[]{:S(2)}, u32[]{:S(2)}) async-start(f32[16,40,256]{2,1,0:T(8,128)} %pack.1), calls=%async_computation | async-start | bytes 1310720 | tf_op jit(solution)/shard_map/all_to_all | solution.py:537
  10.0 0.1 pad_add_fusion.place_ref
  10.1 10.2 %all-to-all-done.all_ref = f32[16,40,256]{2,1,0:T(8,128)S(1)} async-done(((f32[16,40,256]{2,1,0:T(8,128)}), f32[16,40,256]{2,1,0:T(8,128)S(1)}, u32[]{:S(2)}, u32[]{:S(2)}) %all-to-all-start) | async-done | bytes 655392 | tf_op jit(solution)/shard_map/all_to_all | solution.py:537
  20.2 1.3 %pick.1 = (f32[180,256]{1,0:T(8,128)S(1)}, f32[32,1,640]{2,1,0:T(1,128)}) custom-call(s32[3]{0:T(128)S(1)} %pad_add_fusion.place_ref, f32[16,40,256]{2,1,0:T(8,128)S(1)} %all-to-all-done.all_ref), custom_call_target="tpu_custom_call" | custom-call | tf_op jit(solution)/shard_map/pick/pallas_call | solution.py:538
  21.6 5.6 %collective-permute-start.1 = (f32[180,256]{1,0:T(8,128)S(1)}, f32[180,256]{1,0:T(8,128)S(1)}, u32[]{:S(2)}, u32[]{:S(2)}) collective-permute-start(f32[180,256]{1,0:T(8,128)S(1)} %get-tuple-element.8.middle_ref.sheet_ref), channel_id=1, source_target_pairs={{1,0},{2,1},{3,2},{4,3},{5,4},{6,5},{7,6},{8,7},{9,8},{10,9},{11,1... | collective-permute-start | bytes 552968 | tf_op jit(solution)/shard_map/ppermute | solution.py:512
  27.2 3.4 %collective-permute-start = (f32[180,256]{1,0:T(8,128)S(1)}, f32[180,256]{1,0:T(8,128)S(1)}, u32[]{:S(2)}, u32[]{:S(2)}) collective-permute-start(f32[180,256]{1,0:T(8,128)S(1)} %get-tuple-element.8.middle_ref.sheet_ref), channel_id=1, source_target_pairs={{0,1},{1,2},{2,3},{3,4},{4,5},{5,6},{6,7},{7,8},{8,9},{9,10},{10,1... | collective-permute-start | bytes 552968 | tf_op jit(solution)/shard_map/ppermute | solution.py:512
  30.6 14.5 %all-to-all-start.1 = ((f32[32,1,640]{2,1,0:T(1,128)}), f32[32,1,640]{2,1,0:T(1,128)S(1)}, u32[]{:S(2)}, u32[]{:S(2)}) async-start(f32[32,1,640]{2,1,0:T(1,128)} %get-tuple-element.7), calls=%async_computation.1 | async-start | bytes 163840 | tf_op jit(solution)/shard_map/all_to_all | solution.py:550
  45.1 0.0 copy-start
  45.1 0.0 collective-permute-done.1.after_ref
  45.1 0.0 collective-permute-done.before_ref
  45.1 6.0 %near.1.total = f32[4,8,256]{2,1,0:T(8,128)S(1)} custom-call(f32[180,256]{1,0:T(8,128)S(1)} %collective-permute-done.before_ref, f32[180,256]{1,0:T(8,128)S(1)} %get-tuple-element.8.middle_ref.sheet_ref, f32[180,256]{1,0:T(8,128)S(1)} %collective-permute-done.1.after_ref), custom_call_target="tpu_custom_call" | custom-call | flops 30000001024 | bytes 10000000 | tf_op jit(solution)/shard_map/near/pallas_call | solution.py:358
  51.1 7.7 %all-to-all-done.1.moment_ref = f32[32,1,640]{2,1,0:T(1,128)S(1)} async-done(((f32[32,1,640]{2,1,0:T(1,128)}), f32[32,1,640]{2,1,0:T(1,128)S(1)}, u32[]{:S(2)}, u32[]{:S(2)}) %all-to-all-start.1) | async-done | bytes 81952 | tf_op jit(solution)/shard_map/all_to_all | solution.py:550
  58.8 0.0 copy-done
  58.8 1.6 %far.1 = f32[3,4,1,1,256]{4,3,2,1,0:T(1,128)} custom-call(s32[3]{0:T(128)S(1)} %pad_add_fusion.place_ref, f32[32,1,640]{2,1,0:T(1,128)S(1)} %all-to-all-done.1.moment_ref, f32[3,3]{1,0:T(4,128)S(1)} %copy-done, f32[180,256]{1,0:T(8,128)S(1)} %get-tuple-element.8.middle_ref.sheet_ref, f32[4,8,256]{2,1,0:T(8,128)S(1)} %near.1.total), custom_call_target="tpu_custom_call" | custom-call | tf_op jit(solution)/shard_map/far/pallas_call | solution.py:552
Async XLA Ops:
  2.4 17.8 %all-to-all-start = ((f32[16,40,256]{2,1,0:T(8,128)}), f32[16,40,256]{2,1,0:T(8,128)S(1)}, u32[]{:S(2)}, u32[]{:S(2)}) async-start(f32[16,40,256]{2,1,0:T(8,128)} %pack.1), calls=%async_computation | async-start | bytes 1310720 | tf_op jit(solution)/shard_map/all_to_all | solution.py:537
  21.6 23.5 %collective-permute-start.1 = (f32[180,256]{1,0:T(8,128)S(1)}, f32[180,256]{1,0:T(8,128)S(1)}, u32[]{:S(2)}, u32[]{:S(2)}) collective-permute-start(f32[180,256]{1,0:T(8,128)S(1)} %get-tuple-element.8.middle_ref.sheet_ref), channel_id=1, source_target_pairs={{1,0},{2,1},{3,2},{4,3},{5,4},{6,5},{7,6},{8,7},{9,8},{10,9},{11,1... | collective-permute-start | bytes 552968 | tf_op jit(solution)/shard_map/ppermute | solution.py:512
  27.2 17.9 %collective-permute-start = (f32[180,256]{1,0:T(8,128)S(1)}, f32[180,256]{1,0:T(8,128)S(1)}, u32[]{:S(2)}, u32[]{:S(2)}) collective-permute-start(f32[180,256]{1,0:T(8,128)S(1)} %get-tuple-element.8.middle_ref.sheet_ref), channel_id=1, source_target_pairs={{0,1},{1,2},{2,3},{3,4},{4,5},{5,6},{6,7},{7,8},{8,9},{9,10},{10,1... | collective-permute-start | bytes 552968 | tf_op jit(solution)/shard_map/ppermute | solution.py:512
  30.6 28.2 %all-to-all-start.1 = ((f32[32,1,640]{2,1,0:T(1,128)}), f32[32,1,640]{2,1,0:T(1,128)S(1)}, u32[]{:S(2)}, u32[]{:S(2)}) async-start(f32[32,1,640]{2,1,0:T(1,128)} %get-tuple-element.7), calls=%async_computation.1 | async-start | bytes 163840 | tf_op jit(solution)/shard_map/all_to_all | solution.py:550
  45.1 13.7 %copy-start = (f32[3,3]{1,0:T(4,128)S(1)}, f32[3,3]{1,0:T(4,128)}, u32[]{:S(2)}) copy-start(f32[3,3]{1,0:T(4,128)} %applied_ref.1) | copy-start | bytes 112

commit v5 on v4

--- a/solution.py
+++ b/solution.py
@@ -239,8 +239,8 @@
                 left5[index, :, span] = jnp.concatenate(
                     [value, second, third, jnp.zeros((8, LANES), jnp.float32)], axis=0
                 ).astype(jnp.bfloat16)
-                turned = jnp.transpose(cols[pl.ds(pl.multiple_of(block * 32, 32), 32), :])
-                left_d[index, span, :] = turned.astype(jnp.bfloat16)
+                turned = cols[pl.ds(pl.multiple_of(block * 32, 32), 32), :].astype(jnp.bfloat16)
+                left_d[index, span, :] = jnp.transpose(turned)
         wrap = c + 2 >= steps_ref[j]
         return (
             jnp.where(wrap, jnp.minimum(j + 1, planes - 1), j),
@@ -305,40 +305,39 @@
     weigh(first, buf_a)
     lax.fori_loop(0, lax.shift_right_logical(count + 1, 1), work, first)
 
-    def finish_plane(j, carry):
-        def finish(tile, carry):
-            slot = j * TILES + tile
-            x = [spots[slot, n: n + 1, :] for n in range(3)]
-            both = acc[slot, 0:NUM3, :] + acc[slot, NUM3:2 * NUM3, :]
-            linear = both[18:24] + x[0] * both[0:6] + x[1] * both[6:12] + x[2] * both[12:18]
-            second = acc[slot, 2 * NUM3:, :]
-            v = [
-                x[0] * second[n: n + 1] + x[1] * second[3 + n: 4 + n] + x[2] * second[6 + n: 7 + n]
-                for n in range(3)
-            ]
-            scale = 0.5 * (
-                second[0:1] + second[4:5] + second[8:9]
-                + x[0] * second[9:10] + x[1] * second[10:11] + x[2] * second[11:12]
-            )
-            v = [v[n] + scale * x[n] for n in range(3)]
-            bend = jnp.concatenate([x[a] * v[b] + x[b] * v[a] for a, b in PAIRS], axis=0)
-            value = linear + bend
-            value = jnp.concatenate([value, jnp.zeros((2, CAP), jnp.float32)], axis=0)
-            at = starts_ref[jnp.maximum(j - 2, 0)] + CAP * tile
-            low = jnp.bitwise_and(at, LANES - 1)
-            place = pl.multiple_of(lax.shift_right_logical(at, 7) * 8, 8)
-            keep = lane[0:8] >= low
-            one = pltpu.roll(value[:, 0:LANES], low, 1)
-            two = pltpu.roll(value[:, LANES:], low, 1)
-            total[pl.ds(place, 8), :] += jnp.where(keep, one, 0.0)
-            total[pl.ds(place + 8, 8), :] += jnp.where(keep, two, one)
-            total[pl.ds(place + 16, 8), :] += jnp.where(keep, 0.0, two)
-            return carry
-
-        lax.fori_loop(0, tiles_ref[j], finish, 0)
-        return carry
-
-    lax.fori_loop(0, planes, finish_plane, 0)
+    def finish(j, tile):
+        slot = j * TILES + tile
+        x = [spots[slot, n: n + 1, :] for n in range(3)]
+        both = acc[slot, 0:NUM3, :] + acc[slot, NUM3:2 * NUM3, :]
+        linear = both[18:24] + x[0] * both[0:6] + x[1] * both[6:12] + x[2] * both[12:18]
+        second = acc[slot, 2 * NUM3:, :]
+        v = [
+            x[0] * second[n: n + 1] + x[1] * second[3 + n: 4 + n] + x[2] * second[6 + n: 7 + n]
+            for n in range(3)
+        ]
+        scale = 0.5 * (
+            second[0:1] + second[4:5] + second[8:9]
+            + x[0] * second[9:10] + x[1] * second[10:11] + x[2] * second[11:12]
+        )
+        v = [v[n] + scale * x[n] for n in range(3)]
+        bend = jnp.concatenate([x[a] * v[b] + x[b] * v[a] for a, b in PAIRS], axis=0)
+        value = linear + bend
+        value = jnp.concatenate([value, jnp.zeros((2, CAP), jnp.float32)], axis=0)
+        at = starts_ref[max(j - 2, 0)] + CAP * tile
+        low = jnp.bitwise_and(at, LANES - 1)
+        place = pl.multiple_of(lax.shift_right_logical(at, 7) * 8, 8)
+        keep = lane[0:8] >= low
+        one = pltpu.roll(value[:, 0:LANES], low, 1)
+        two = pltpu.roll(value[:, LANES:], low, 1)
+        total[pl.ds(place, 8), :] += jnp.where(keep, one, 0.0)
+        total[pl.ds(place + 8, 8), :] += jnp.where(keep, two, one)
+        total[pl.ds(place + 16, 8), :] += jnp.where(keep, 0.0, two)
+
+    for j in range(planes):
+        finish(j, 0)
+    for j in range(planes):
+        for tile in range(1, min(j, cells - 1) + 1 - max(j - 2, 0)):
+            pl.when(tile < tiles_ref[j])(functools.partial(finish, j, tile))
 
     for i in range(cells):
         at = starts_ref[i]
@@ -385,7 +384,7 @@
     )(before, sheet, after)
 
 
-def far_kernel(planes, spans, place_ref, moment_ref, applied_ref, sheet_ref, total, out_ref):
+def far_kernel(planes, spans, moment_ref, applied_ref, sheet_ref, total, out_ref):
     cells = planes - 2
     span_x, span_y, span_z = spans
     shape = (span_z, LANES)
@@ -407,8 +406,9 @@
     index = {}
     for n, (a, b) in enumerate(PAIRS):
         index[a, b] = index[b, a] = n
+    pieces = []
     for i in range(cells):
-        mine = (place_ref[0] * cells + i, place_ref[1], place_ref[2])
+        mine = (lax.axis_index("gx") * cells + i, lax.axis_index("gy"), lax.axis_index("gz"))
         r = [mine[n].astype(jnp.float32) - source[n] for n in range(3)]
         reach = jnp.maximum(jnp.maximum(jnp.abs(r[0]), jnp.abs(r[1])), jnp.abs(r[2]))
         inv = lax.rsqrt(r[0] * r[0] + r[1] * r[1] + r[2] * r[2] + CORE_SQUARE)
@@ -422,7 +422,6 @@
         cut = SECOND * cube
         bulk = SECOND * along * (radial - cube)
         front = -FIRST * radial
-        stress = []
         for n, (a, b) in enumerate(PAIRS):
             element = (
                 front * (turn[b][a] + turn[a][b])
@@ -431,9 +430,18 @@
             )
             if a == b:
                 element = element + bulk
+            pieces.append(plus([element[k: k + 8] for k in range(0, span_z, 8)]))
+    pieces = [
+        jnp.sum(jnp.sum(jnp.swapaxes(jnp.stack(pieces[k: k + 8]), 0, 1), axis=0), axis=1, keepdims=True)
+        for k in range(0, len(pieces), 8)
+    ]
+    for i in range(cells):
+        stress = []
+        for n, (a, b) in enumerate(PAIRS):
+            k = 6 * i + n
             stress.append(
-                jnp.sum(element, axis=(0, 1), keepdims=True)
-                + 0.5 * (applied_ref[a, b] + applied_ref[b, a])
+                pieces[k // 8][k % 8: k % 8 + 1]
+                + 0.5 * (applied_ref[a: a + 1, b: b + 1] + applied_ref[b: b + 1, a: a + 1])
                 + total[i, n: n + 1, :]
             )
         row = ROWS * (planes + 1 + i)
@@ -444,19 +452,22 @@
             out_ref[n, i, 0, :, :] = value
 
 
-def pack_kernel(counts_ref, offset_ref, vector_ref, burgers_ref, all_ref, hold, sems):
+def pack_kernel(counts_ref, offset_ref, vector_ref, burgers_ref, all_ref, hold, count_hold, sems):
     cells = offset_ref.shape[1]
     copies = [
         pltpu.make_async_copy(ref, hold.at[n], sems.at[n])
         for n, ref in enumerate((offset_ref, vector_ref, burgers_ref))
     ]
+    number = pltpu.make_async_copy(counts_ref, count_hold, sems.at[3])
+    number.start()
     for copy in copies:
         copy.start()
+    number.wait()
     slot = lax.broadcasted_iota(jnp.int32, (cells, CAP), 1)
     cell = lax.broadcasted_iota(jnp.int32, (cells, CAP), 0)
     live = jnp.zeros((cells, CAP), jnp.int32)
     for i in range(cells):
-        live = jnp.where(cell == i, counts_ref[i], live)
+        live = jnp.where(cell == i, count_hold[i], live)
     filled = slot < live
     for copy in copies:
         copy.wait()
@@ -475,15 +486,15 @@
         all_ref[d] = packed
 
 
-def pick_kernel(planes, spans, place_ref, all_ref, sheet_ref, moment_ref):
+def pick_kernel(planes, spans, all_ref, sheet_ref, moment_ref):
     span_x, span_y, span_z = spans
     cells = planes - 2
     for dy in range(3):
-        y = place_ref[1] + (dy - 1)
+        y = lax.axis_index("gy") + (dy - 1)
         for j in range(planes):
             step = (j + cells - 1) // cells - 1
             c = (j - 1) % cells
-            x = place_ref[0] + step
+            x = lax.axis_index("gx") + step
             inside = (x >= 0) & (x < span_x) & (y >= 0) & (y < span_y)
             device = jnp.clip(x, 0, span_x - 1) * span_y + jnp.clip(y, 0, span_y - 1)
             row = ROWS * (dy * planes + j)
@@ -516,20 +527,19 @@
     cells = seg_offset.shape[1]
     planes = cells + 2
     spans = tuple(lax.axis_size(a) for a in ("gx", "gy", "gz"))
-    place = jnp.stack([lax.axis_index(a) for a in ("gx", "gy", "gz")]).astype(jnp.int32)
     devices = spans[0] * spans[1]
     vmem = pl.BlockSpec(memory_space=pltpu.VMEM)
-    smem = pl.BlockSpec(memory_space=pltpu.SMEM)
     anywhere = pl.BlockSpec(memory_space=pl.ANY)
     limit = pltpu.CompilerParams(vmem_limit_bytes=40 * 1024 * 1024)
     packed = pl.pallas_call(
         pack_kernel,
         out_shape=jax.ShapeDtypeStruct((devices, cells * ROWS, CAP), jnp.float32),
-        in_specs=[smem] + [anywhere] * 3,
+        in_specs=[anywhere] * 4,
         out_specs=vmem,
         scratch_shapes=[
             pltpu.VMEM((3,) + seg_offset.shape, jnp.float32),
-            pltpu.SemaphoreType.DMA((3,)),
+            pltpu.SMEM((cells,), jnp.int32),
+            pltpu.SemaphoreType.DMA((4,)),
         ],
         compiler_params=pltpu.CompilerParams(vmem_limit_bytes=60 * 1024 * 1024),
         name="pack",
@@ -541,22 +551,22 @@
             jax.ShapeDtypeStruct((3 * planes * ROWS, CAP), jnp.float32),
             jax.ShapeDtypeStruct((spans[2], 1, 5 * LANES), jnp.float32),
         ),
-        in_specs=[smem, vmem],
+        in_specs=[vmem],
         out_specs=(vmem, vmem),
         compiler_params=limit,
         name="pick",
-    )(place, every)
+    )(every)
     before, after = beside(sheet, sheet, "gz")
     moments = lax.all_to_all(moments, "gz", 0, 0)
     total = near_call(before, sheet, after)
     return pl.pallas_call(
         functools.partial(far_kernel, planes, spans),
         out_shape=jax.ShapeDtypeStruct(seg_offset.shape, jnp.float32),
-        in_specs=[smem, vmem, smem, vmem, vmem],
+        in_specs=[vmem] * 4,
         out_specs=vmem,
         compiler_params=limit,
         name="far",
-    )(place, moments, applied, sheet, total)
+    )(moments, applied, sheet, total)
 
 
 def solution(mesh):

time: 60.8 us -> 59 us (0.970)
  blocking collectives: 0 us -> 17.8 us
  waiting for transfers between devices: 17.8 us -> 4.01 us
  starting transfers between devices: 31.1 us -> 23.5 us
  Pallas kernels: 11.3 us -> 13.3 us
    all_to_all x0 -> x1, blocking collectives: none -> 17.8 us  [local(): every = lax.all_to_all(packed, ('gx', 'gy'), 0, 0)]
    all_to_all x1 -> x0, waiting for transfers between devices: 10.2 us -> none  [local(): every = lax.all_to_all(packed, ('gx', 'gy'), 0, 0)]
    all_to_all x1 -> x0, starting transfers between devices: 7.6 us -> none  [local(): every = lax.all_to_all(packed, ('gx', 'gy'), 0, 0)]
    all_to_all x1, waiting for transfers between devices: 7.65 us -> 4 us  [local(): moments = lax.all_to_all(moments, 'gz', 0, 0)]
    pallas_call x1, Pallas kernels: 6.02 us -> 9.67 us  [near_call(): pl.pallas_call(functools.partial(near_kernel, planes), out_shape=jax.Shap...]
    pallas_call x1, Pallas kernels: 2.38 us -> 1.73 us  [local(): pl.pallas_call(pack_kernel, out_shape=jax.ShapeDtypeStruct((devices, cell...]
  transfers between devices with their start and end apart: 4 -> 3, of which waited for: 2 -> 1; matrix products, arithmetic and copies ran while one was open for 0% -> 0% of each run, Pallas kernels for 10% -> 16%
where the time goes in v5:
time: 59 us; the launch traced here: 58.7 us
  starting transfers between devices  23.5 us (40%)
  blocking collectives  17.8 us (30%)
  Pallas kernels  13.3 us (23%)
  waiting for transfers between devices  4.01 us (7%)
    all_to_all x1, blocking collectives, local(): every = lax.all_to_all(packed, ('gx', 'gy'), 0, 0)  17.8 us
    all_to_all x1, starting transfers between devices, local(): moments = lax.all_to_all(moments, 'gz', 0, 0)  14.5 us
    pallas_call x1, Pallas kernels, near_call(): pl.pallas_call(functools.partial(near_kernel, planes), out_shape=jax.Shap...  9.67 us
    ppermute x2, starting transfers between devices, beside(): return (lax.ppermute(last, axis, up), lax.ppermute(first, axis, down))  9.06 us
    all_to_all x1, waiting for transfers between devices, local(): moments = lax.all_to_all(moments, 'gz', 0, 0)  4 us
    pallas_call x1, Pallas kernels, local(): pl.pallas_call(pack_kernel, out_shape=jax.ShapeDtypeStruct((devices, cell...  1.73 us
  transfers between devices with their start and end apart: 3, of which 1 were waited for; matrix products, arithmetic and copies ran while one was open for 0% of the time, Pallas kernels for 16%

profile of v5, /device:TPU:1, one launch (start us, length us, event | category | flops | bytes accessed | tf_op | source)
XLA Modules:
  0.0 58.7 jit_solution(8757726839896199586)
XLA Ops:
  0.0 1.7 %pack.1 = f32[16,40,256]{2,1,0:T(8,128)} custom-call(s32[4]{0:T(128)} %bitcast.1, f32[3,4,1,1,256]{4,3,2,1,0:T(1,128)} %offset_ref.1, f32[3,4,1,1,256]{4,3,2,1,0:T(1,128)} %vector_ref.1, f32[3,4,1,1,256]{4,3,2,1,0:T(1,128)} %burgers_ref.1), custom_call_target="tpu_custom_call" | custom-call | tf_op jit(solution)/shard_map/pack/pallas_call | solution.py:534
  1.7 17.8 %all_to_all.10.all_ref = f32[16,40,256]{2,1,0:T(8,128)S(1)} all-to-all(f32[16,40,256]{2,1,0:T(8,128)} %pack.1), channel_id=1, replica_groups=mesh['gx'=4,'gy'=4,'gz'=32] {'gx','gy'}, dimensions={0} | all-to-all | bytes 1310720 | tf_op jit(solution)/shard_map/all_to_all | solution.py:547
  19.5 0.8 %pick.1 = (f32[180,256]{1,0:T(8,128)S(1)}, f32[32,1,640]{2,1,0:T(1,128)}) custom-call(f32[16,40,256]{2,1,0:T(8,128)S(1)} %all_to_all.10.all_ref), custom_call_target="tpu_custom_call" | custom-call | tf_op jit(solution)/shard_map/pick/pallas_call | solution.py:548
  20.3 5.6 %collective-permute-start.1 = (f32[180,256]{1,0:T(8,128)S(1)}, f32[180,256]{1,0:T(8,128)S(1)}, u32[]{:S(2)}, u32[]{:S(2)}) collective-permute-start(f32[180,256]{1,0:T(8,128)S(1)} %get-tuple-element.8.middle_ref.sheet_ref), channel_id=1, source_target_pairs={{1,0},{2,1},{3,2},{4,3},{5,4},{6,5},{7,6},{8,7},{9,8},{10,9},{11,1... | collective-permute-start | bytes 552968 | tf_op jit(solution)/shard_map/ppermute | solution.py:523
  25.9 3.4 %collective-permute-start = (f32[180,256]{1,0:T(8,128)S(1)}, f32[180,256]{1,0:T(8,128)S(1)}, u32[]{:S(2)}, u32[]{:S(2)}) collective-permute-start(f32[180,256]{1,0:T(8,128)S(1)} %get-tuple-element.8.middle_ref.sheet_ref), channel_id=1, source_target_pairs={{0,1},{1,2},{2,3},{3,4},{4,5},{5,6},{6,7},{7,8},{8,9},{9,10},{10,1... | collective-permute-start | bytes 552968 | tf_op jit(solution)/shard_map/ppermute | solution.py:523
  29.4 14.5 %all-to-all-start.1 = ((f32[32,1,640]{2,1,0:T(1,128)}), f32[32,1,640]{2,1,0:T(1,128)S(1)}, u32[]{:S(2)}, u32[]{:S(2)}) async-start(f32[32,1,640]{2,1,0:T(1,128)} %get-tuple-element.7), calls=%async_computation.1 | async-start | bytes 163840 | tf_op jit(solution)/shard_map/all_to_all | solution.py:560
  43.9 0.0 copy-start
  43.9 0.0 collective-permute-done.1.after_ref
  43.9 0.0 collective-permute-done.before_ref
  43.9 9.7 %near.1.total = f32[4,8,256]{2,1,0:T(8,128)S(1)} custom-call(f32[180,256]{1,0:T(8,128)S(1)} %collective-permute-done.before_ref, f32[180,256]{1,0:T(8,128)S(1)} %get-tuple-element.8.middle_ref.sheet_ref, f32[180,256]{1,0:T(8,128)S(1)} %collective-permute-done.1.after_ref), custom_call_target="tpu_custom_call" | custom-call | flops 30000001024 | bytes 10000000 | tf_op jit(solution)/shard_map/near/pallas_call | solution.py:357
  53.6 4.0 %all-to-all-done.1.moment_ref = f32[32,1,640]{2,1,0:T(1,128)S(1)} async-done(((f32[32,1,640]{2,1,0:T(1,128)}), f32[32,1,640]{2,1,0:T(1,128)S(1)}, u32[]{:S(2)}, u32[]{:S(2)}) %all-to-all-start.1) | async-done | bytes 81952 | tf_op jit(solution)/shard_map/all_to_all | solution.py:560
  57.6 0.0 copy-done
  57.6 1.1 %far.1 = f32[3,4,1,1,256]{4,3,2,1,0:T(1,128)} custom-call(f32[32,1,640]{2,1,0:T(1,128)S(1)} %all-to-all-done.1.moment_ref, f32[3,3]{1,0:T(4,128)S(1)} %copy-done, f32[180,256]{1,0:T(8,128)S(1)} %get-tuple-element.8.middle_ref.sheet_ref, f32[4,8,256]{2,1,0:T(8,128)S(1)} %near.1.total), custom_call_target="tpu_custom_call" | custom-call | tf_op jit(solution)/shard_map/far/pallas_call | solution.py:562
Async XLA Ops:
  20.3 23.6 %collective-permute-start.1 = (f32[180,256]{1,0:T(8,128)S(1)}, f32[180,256]{1,0:T(8,128)S(1)}, u32[]{:S(2)}, u32[]{:S(2)}) collective-permute-start(f32[180,256]{1,0:T(8,128)S(1)} %get-tuple-element.8.middle_ref.sheet_ref), channel_id=1, source_target_pairs={{1,0},{2,1},{3,2},{4,3},{5,4},{6,5},{7,6},{8,7},{9,8},{10,9},{11,1... | collective-permute-start | bytes 552968 | tf_op jit(solution)/shard_map/ppermute | solution.py:523
  25.9 18.0 %collective-permute-start = (f32[180,256]{1,0:T(8,128)S(1)}, f32[180,256]{1,0:T(8,128)S(1)}, u32[]{:S(2)}, u32[]{:S(2)}) collective-permute-start(f32[180,256]{1,0:T(8,128)S(1)} %get-tuple-element.8.middle_ref.sheet_ref), channel_id=1, source_target_pairs={{0,1},{1,2},{2,3},{3,4},{4,5},{5,6},{6,7},{7,8},{8,9},{9,10},{10,1... | collective-permute-start | bytes 552968 | tf_op jit(solution)/shard_map/ppermute | solution.py:523
  29.4 28.2 %all-to-all-start.1 = ((f32[32,1,640]{2,1,0:T(1,128)}), f32[32,1,640]{2,1,0:T(1,128)S(1)}, u32[]{:S(2)}, u32[]{:S(2)}) async-start(f32[32,1,640]{2,1,0:T(1,128)} %get-tuple-element.7), calls=%async_computation.1 | async-start | bytes 163840 | tf_op jit(solution)/shard_map/all_to_all | solution.py:560
  43.9 13.7 %copy-start = (f32[3,3]{1,0:T(4,128)S(1)}, f32[3,3]{1,0:T(4,128)}, u32[]{:S(2)}) copy-start(f32[3,3]{1,0:T(4,128)} %applied_ref.1) | copy-start | bytes 112

commit v6 on v5

--- a/solution.py
+++ b/solution.py
@@ -137,6 +137,8 @@
             first = sources[k][row: row + ROWS, 0:LANES]
             second = sources[k][row: row + ROWS, LANES:]
             count = first[ROWS - 1: ROWS, 0:1].astype(jnp.int32)[0, 0]
+            if k == 0:
+                count = jnp.where(lax.axis_index("gz") == 0, 0, count)
             if k == 1 and c == 1 and 0 < j < planes - 1:
                 shift = jnp.where(lift[0:8] == 0, j - 0.5, -0.5)
                 mark = lift[0:8] < 3
@@ -518,7 +520,7 @@
 
 def beside(first, last, axis):
     devices = lax.axis_size(axis)
-    up = [(i, i + 1) for i in range(devices - 1)]
+    up = [(i, (i + 1) % devices) for i in range(devices)]
     down = [(i + 1, i) for i in range(devices - 1)]
     return lax.ppermute(last, axis, up), lax.ppermute(first, axis, down)
 

time: 59 us -> 57.1 us (0.968)
  Pallas kernels: 13.3 us -> 8.99 us
  waiting for transfers between devices: 4.01 us -> 8.31 us
  starting transfers between devices: 23.5 us -> 21.6 us
    all_to_all x1, waiting for transfers between devices: 4 us -> 8.3 us  [local(): moments = lax.all_to_all(moments, 'gz', 0, 0)]
    pallas_call x1, Pallas kernels: 9.67 us -> 5.37 us  [near_call(): pl.pallas_call(functools.partial(near_kernel, planes), out_shape=jax.Shap...]
    ppermute x2, starting transfers between devices: 9.06 us -> 7.16 us  [beside(): return (lax.ppermute(last, axis, up), lax.ppermute(first, axis, down))]
  transfers between devices with their start and end apart: 3 -> 3, of which waited for: 1 -> 1; matrix products, arithmetic and copies ran while one was open for 0% -> 0% of each run, Pallas kernels for 16% -> 9%
where the time goes in v6:
time: 57.1 us; the launch traced here: 56.8 us
  starting transfers between devices  21.6 us (38%)
  blocking collectives  17.8 us (31%)
  Pallas kernels  8.99 us (16%)
  waiting for transfers between devices  8.31 us (15%)
    all_to_all x1, blocking collectives, local(): every = lax.all_to_all(packed, ('gx', 'gy'), 0, 0)  17.8 us
    all_to_all x1, starting transfers between devices, local(): moments = lax.all_to_all(moments, 'gz', 0, 0)  14.5 us
    all_to_all x1, waiting for transfers between devices, local(): moments = lax.all_to_all(moments, 'gz', 0, 0)  8.3 us
    ppermute x2, starting transfers between devices, beside(): return (lax.ppermute(last, axis, up), lax.ppermute(first, axis, down))  7.16 us
    pallas_call x1, Pallas kernels, near_call(): pl.pallas_call(functools.partial(near_kernel, planes), out_shape=jax.Shap...  5.37 us
    pallas_call x1, Pallas kernels, local(): pl.pallas_call(pack_kernel, out_shape=jax.ShapeDtypeStruct((devices, cell...  1.73 us
  transfers between devices with their start and end apart: 3, of which 1 were waited for; matrix products, arithmetic and copies ran while one was open for 0% of the time, Pallas kernels for 9%

profile of v6, /device:TPU:1, one launch (start us, length us, event | category | flops | bytes accessed | tf_op | source)
XLA Modules:
  0.0 56.8 jit_solution(709613779595570321)
XLA Ops:
  0.0 1.7 %pack.1 = f32[16,40,256]{2,1,0:T(8,128)} custom-call(s32[4]{0:T(128)} %bitcast.1, f32[3,4,1,1,256]{4,3,2,1,0:T(1,128)} %offset_ref.1, f32[3,4,1,1,256]{4,3,2,1,0:T(1,128)} %vector_ref.1, f32[3,4,1,1,256]{4,3,2,1,0:T(1,128)} %burgers_ref.1), custom_call_target="tpu_custom_call" | custom-call | tf_op jit(solution)/shard_map/pack/pallas_call | solution.py:536
  1.7 17.8 %all_to_all.10.all_ref = f32[16,40,256]{2,1,0:T(8,128)S(1)} all-to-all(f32[16,40,256]{2,1,0:T(8,128)} %pack.1), channel_id=1, replica_groups=mesh['gx'=4,'gy'=4,'gz'=32] {'gx','gy'}, dimensions={0} | all-to-all | bytes 1310720 | tf_op jit(solution)/shard_map/all_to_all | solution.py:549
  19.5 0.8 %pick.1 = (f32[180,256]{1,0:T(8,128)S(1)}, f32[32,1,640]{2,1,0:T(1,128)}) custom-call(f32[16,40,256]{2,1,0:T(8,128)S(1)} %all_to_all.10.all_ref), custom_call_target="tpu_custom_call" | custom-call | tf_op jit(solution)/shard_map/pick/pallas_call | solution.py:550
  20.3 5.6 %collective-permute-start.1 = (f32[180,256]{1,0:T(8,128)S(1)}, f32[180,256]{1,0:T(8,128)S(1)}, u32[]{:S(2)}, u32[]{:S(2)}) collective-permute-start(f32[180,256]{1,0:T(8,128)S(1)} %get-tuple-element.8.middle_ref.sheet_ref), channel_id=1, source_target_pairs={{1,0},{2,1},{3,2},{4,3},{5,4},{6,5},{7,6},{8,7},{9,8},{10,9},{11,1... | collective-permute-start | bytes 552968 | tf_op jit(solution)/shard_map/ppermute | solution.py:525
  25.9 1.5 %collective-permute-start = (f32[180,256]{1,0:T(8,128)S(1)}, f32[180,256]{1,0:T(8,128)S(1)}, u32[]{:S(2)}, u32[]{:S(2)}) collective-permute-start(f32[180,256]{1,0:T(8,128)S(1)} %get-tuple-element.8.middle_ref.sheet_ref), channel_id=1, source_target_pairs={{0,1},{1,2},{2,3},{3,4},{4,5},{5,6},{6,7},{7,8},{8,9},{9,10},{10,1... | collective-permute-start | bytes 552968 | tf_op jit(solution)/shard_map/ppermute | solution.py:525
  27.5 14.5 %all-to-all-start.1 = ((f32[32,1,640]{2,1,0:T(1,128)}), f32[32,1,640]{2,1,0:T(1,128)S(1)}, u32[]{:S(2)}, u32[]{:S(2)}) async-start(f32[32,1,640]{2,1,0:T(1,128)} %get-tuple-element.7), calls=%async_computation.1 | async-start | bytes 163840 | tf_op jit(solution)/shard_map/all_to_all | solution.py:562
  41.9 0.0 copy-start
  42.0 0.0 collective-permute-done.1.after_ref
  42.0 0.0 collective-permute-done.before_ref
  42.0 5.4 %near.1.total = f32[4,8,256]{2,1,0:T(8,128)S(1)} custom-call(f32[180,256]{1,0:T(8,128)S(1)} %collective-permute-done.before_ref, f32[180,256]{1,0:T(8,128)S(1)} %get-tuple-element.8.middle_ref.sheet_ref, f32[180,256]{1,0:T(8,128)S(1)} %collective-permute-done.1.after_ref), custom_call_target="tpu_custom_call" | custom-call | flops 30000001024 | bytes 10000000 | tf_op jit(solution)/shard_map/near/pallas_call | solution.py:359
  47.4 8.3 %all-to-all-done.1.moment_ref = f32[32,1,640]{2,1,0:T(1,128)S(1)} async-done(((f32[32,1,640]{2,1,0:T(1,128)}), f32[32,1,640]{2,1,0:T(1,128)S(1)}, u32[]{:S(2)}, u32[]{:S(2)}) %all-to-all-start.1) | async-done | bytes 81952 | tf_op jit(solution)/shard_map/all_to_all | solution.py:562
  55.7 0.0 copy-done
  55.7 1.1 %far.1 = f32[3,4,1,1,256]{4,3,2,1,0:T(1,128)} custom-call(f32[32,1,640]{2,1,0:T(1,128)S(1)} %all-to-all-done.1.moment_ref, f32[3,3]{1,0:T(4,128)S(1)} %copy-done, f32[180,256]{1,0:T(8,128)S(1)} %get-tuple-element.8.middle_ref.sheet_ref, f32[4,8,256]{2,1,0:T(8,128)S(1)} %near.1.total), custom_call_target="tpu_custom_call" | custom-call | tf_op jit(solution)/shard_map/far/pallas_call | solution.py:564
Async XLA Ops:
  20.3 21.7 %collective-permute-start.1 = (f32[180,256]{1,0:T(8,128)S(1)}, f32[180,256]{1,0:T(8,128)S(1)}, u32[]{:S(2)}, u32[]{:S(2)}) collective-permute-start(f32[180,256]{1,0:T(8,128)S(1)} %get-tuple-element.8.middle_ref.sheet_ref), channel_id=1, source_target_pairs={{1,0},{2,1},{3,2},{4,3},{5,4},{6,5},{7,6},{8,7},{9,8},{10,9},{11,1... | collective-permute-start | bytes 552968 | tf_op jit(solution)/shard_map/ppermute | solution.py:525
  25.9 16.0 %collective-permute-start = (f32[180,256]{1,0:T(8,128)S(1)}, f32[180,256]{1,0:T(8,128)S(1)}, u32[]{:S(2)}, u32[]{:S(2)}) collective-permute-start(f32[180,256]{1,0:T(8,128)S(1)} %get-tuple-element.8.middle_ref.sheet_ref), channel_id=1, source_target_pairs={{0,1},{1,2},{2,3},{3,4},{4,5},{5,6},{6,7},{7,8},{8,9},{9,10},{10,1... | collective-permute-start | bytes 552968 | tf_op jit(solution)/shard_map/ppermute | solution.py:525
  27.5 28.2 %all-to-all-start.1 = ((f32[32,1,640]{2,1,0:T(1,128)}), f32[32,1,640]{2,1,0:T(1,128)S(1)}, u32[]{:S(2)}, u32[]{:S(2)}) async-start(f32[32,1,640]{2,1,0:T(1,128)} %get-tuple-element.7), calls=%async_computation.1 | async-start | bytes 163840 | tf_op jit(solution)/shard_map/all_to_all | solution.py:562
  41.9 13.7 %copy-start = (f32[3,3]{1,0:T(4,128)S(1)}, f32[3,3]{1,0:T(4,128)}, u32[]{:S(2)}) copy-start(f32[3,3]{1,0:T(4,128)} %applied_ref.1) | copy-start | bytes 112

commit v7 on v6

--- a/solution.py
+++ b/solution.py
@@ -110,7 +110,7 @@
 ):
     sources = (before_ref, middle_ref, after_ref)
     cells = planes - 2
-    columns = [(k, c) for k in range(3) for c in range(3)]
+    columns = [(k, c) for k in (0, 2, 1) for c in range(3)]
     lane = lax.broadcasted_iota(jnp.int32, (16, LANES), 1)
     lift = lax.broadcasted_iota(jnp.int32, (16, LANES), 0)
     mm = functools.partial(jnp.dot, preferred_element_type=jnp.float32)
@@ -137,8 +137,9 @@
             first = sources[k][row: row + ROWS, 0:LANES]
             second = sources[k][row: row + ROWS, LANES:]
             count = first[ROWS - 1: ROWS, 0:1].astype(jnp.int32)[0, 0]
-            if k == 0:
-                count = jnp.where(lax.axis_index("gz") == 0, 0, count)
+            if k != 1:
+                edge = 0 if k == 0 else lax.axis_size("gz") - 1
+                count = jnp.where(lax.axis_index("gz") == edge, 0, count)
             if k == 1 and c == 1 and 0 < j < planes - 1:
                 shift = jnp.where(lift[0:8] == 0, j - 0.5, -0.5)
                 mark = lift[0:8] < 3
@@ -521,7 +522,7 @@
 def beside(first, last, axis):
     devices = lax.axis_size(axis)
     up = [(i, (i + 1) % devices) for i in range(devices)]
-    down = [(i + 1, i) for i in range(devices - 1)]
+    down = [((i + 1) % devices, i) for i in range(devices)]
     return lax.ppermute(last, axis, up), lax.ppermute(first, axis, down)
 
 

time: 57.1 us -> 55.1 us (0.965)
  starting transfers between devices: 21.6 us -> 19.7 us
    ppermute x2, starting transfers between devices: 7.16 us -> 5.24 us  [beside(): return (lax.ppermute(last, axis, up), lax.ppermute(first, axis, down))]
where the time goes in v7:
time: 55.1 us; the launch traced here: 54.8 us
  starting transfers between devices  19.7 us (36%)
  blocking collectives  17.8 us (32%)
  waiting for transfers between devices  8.76 us (16%)
  Pallas kernels  8.55 us (16%)
    all_to_all x1, blocking collectives, local(): every = lax.all_to_all(packed, ('gx', 'gy'), 0, 0)  17.8 us
    all_to_all x1, starting transfers between devices, local(): moments = lax.all_to_all(moments, 'gz', 0, 0)  14.5 us
    all_to_all x1, waiting for transfers between devices, local(): moments = lax.all_to_all(moments, 'gz', 0, 0)  8.75 us
    ppermute x2, starting transfers between devices, beside(): return (lax.ppermute(last, axis, up), lax.ppermute(first, axis, down))  5.24 us
    pallas_call x1, Pallas kernels, near_call(): pl.pallas_call(functools.partial(near_kernel, planes), out_shape=jax.Shap...  4.92 us
    pallas_call x1, Pallas kernels, local(): pl.pallas_call(pack_kernel, out_shape=jax.ShapeDtypeStruct((devices, cell...  1.73 us
  transfers between devices with their start and end apart: 3, of which 1 were waited for; matrix products, arithmetic and copies ran while one was open for 0% of the time, Pallas kernels for 9%

profile of v7, /device:TPU:1, one launch (start us, length us, event | category | flops | bytes accessed | tf_op | source)
XLA Modules:
  0.0 54.8 jit_solution(15657875584883212884)
XLA Ops:
  0.0 1.7 %pack.1 = f32[16,40,256]{2,1,0:T(8,128)} custom-call(s32[4]{0:T(128)} %bitcast.1, f32[3,4,1,1,256]{4,3,2,1,0:T(1,128)} %offset_ref.1, f32[3,4,1,1,256]{4,3,2,1,0:T(1,128)} %vector_ref.1, f32[3,4,1,1,256]{4,3,2,1,0:T(1,128)} %burgers_ref.1), custom_call_target="tpu_custom_call" | custom-call | tf_op jit(solution)/shard_map/pack/pallas_call | solution.py:537
  1.7 17.8 %all_to_all.10.all_ref = f32[16,40,256]{2,1,0:T(8,128)S(1)} all-to-all(f32[16,40,256]{2,1,0:T(8,128)} %pack.1), channel_id=1, replica_groups=mesh['gx'=4,'gy'=4,'gz'=32] {'gx','gy'}, dimensions={0} | all-to-all | bytes 1310720 | tf_op jit(solution)/shard_map/all_to_all | solution.py:550
  19.5 0.8 %pick.1 = (f32[180,256]{1,0:T(8,128)S(1)}, f32[32,1,640]{2,1,0:T(1,128)}) custom-call(f32[16,40,256]{2,1,0:T(8,128)S(1)} %all_to_all.10.all_ref), custom_call_target="tpu_custom_call" | custom-call | tf_op jit(solution)/shard_map/pick/pallas_call | solution.py:551
  20.3 3.7 %collective-permute-start.1 = (f32[180,256]{1,0:T(8,128)S(1)}, f32[180,256]{1,0:T(8,128)S(1)}, u32[]{:S(2)}, u32[]{:S(2)}) collective-permute-start(f32[180,256]{1,0:T(8,128)S(1)} %get-tuple-element.8.middle_ref.sheet_ref), channel_id=1, source_target_pairs={{1,0},{2,1},{3,2},{4,3},{5,4},{6,5},{7,6},{8,7},{9,8},{10,9},{11,1... | collective-permute-start | bytes 552968 | tf_op jit(solution)/shard_map/ppermute | solution.py:526
  24.0 1.5 %collective-permute-start = (f32[180,256]{1,0:T(8,128)S(1)}, f32[180,256]{1,0:T(8,128)S(1)}, u32[]{:S(2)}, u32[]{:S(2)}) collective-permute-start(f32[180,256]{1,0:T(8,128)S(1)} %get-tuple-element.8.middle_ref.sheet_ref), channel_id=1, source_target_pairs={{0,1},{1,2},{2,3},{3,4},{4,5},{5,6},{6,7},{7,8},{8,9},{9,10},{10,1... | collective-permute-start | bytes 552968 | tf_op jit(solution)/shard_map/ppermute | solution.py:526
  25.6 14.5 %all-to-all-start.1 = ((f32[32,1,640]{2,1,0:T(1,128)}), f32[32,1,640]{2,1,0:T(1,128)S(1)}, u32[]{:S(2)}, u32[]{:S(2)}) async-start(f32[32,1,640]{2,1,0:T(1,128)} %get-tuple-element.7), calls=%async_computation.1 | async-start | bytes 163840 | tf_op jit(solution)/shard_map/all_to_all | solution.py:563
  40.0 0.0 copy-start
  40.0 0.0 collective-permute-done.1.after_ref
  40.0 0.0 collective-permute-done.before_ref
  40.1 4.9 %near.1.total = f32[4,8,256]{2,1,0:T(8,128)S(1)} custom-call(f32[180,256]{1,0:T(8,128)S(1)} %collective-permute-done.before_ref, f32[180,256]{1,0:T(8,128)S(1)} %get-tuple-element.8.middle_ref.sheet_ref, f32[180,256]{1,0:T(8,128)S(1)} %collective-permute-done.1.after_ref), custom_call_target="tpu_custom_call" | custom-call | flops 30000001024 | bytes 10000000 | tf_op jit(solution)/shard_map/near/pallas_call | solution.py:360
  45.0 8.8 %all-to-all-done.1.moment_ref = f32[32,1,640]{2,1,0:T(1,128)S(1)} async-done(((f32[32,1,640]{2,1,0:T(1,128)}), f32[32,1,640]{2,1,0:T(1,128)S(1)}, u32[]{:S(2)}, u32[]{:S(2)}) %all-to-all-start.1) | async-done | bytes 81952 | tf_op jit(solution)/shard_map/all_to_all | solution.py:563
  53.7 0.0 copy-done
  53.7 1.1 %far.1 = f32[3,4,1,1,256]{4,3,2,1,0:T(1,128)} custom-call(f32[32,1,640]{2,1,0:T(1,128)S(1)} %all-to-all-done.1.moment_ref, f32[3,3]{1,0:T(4,128)S(1)} %copy-done, f32[180,256]{1,0:T(8,128)S(1)} %get-tuple-element.8.middle_ref.sheet_ref, f32[4,8,256]{2,1,0:T(8,128)S(1)} %near.1.total), custom_call_target="tpu_custom_call" | custom-call | tf_op jit(solution)/shard_map/far/pallas_call | solution.py:565
Async XLA Ops:
  20.3 19.7 %collective-permute-start.1 = (f32[180,256]{1,0:T(8,128)S(1)}, f32[180,256]{1,0:T(8,128)S(1)}, u32[]{:S(2)}, u32[]{:S(2)}) collective-permute-start(f32[180,256]{1,0:T(8,128)S(1)} %get-tuple-element.8.middle_ref.sheet_ref), channel_id=1, source_target_pairs={{1,0},{2,1},{3,2},{4,3},{5,4},{6,5},{7,6},{8,7},{9,8},{10,9},{11,1... | collective-permute-start | bytes 552968 | tf_op jit(solution)/shard_map/ppermute | solution.py:526
  24.0 16.0 %collective-permute-start = (f32[180,256]{1,0:T(8,128)S(1)}, f32[180,256]{1,0:T(8,128)S(1)}, u32[]{:S(2)}, u32[]{:S(2)}) collective-permute-start(f32[180,256]{1,0:T(8,128)S(1)} %get-tuple-element.8.middle_ref.sheet_ref), channel_id=1, source_target_pairs={{0,1},{1,2},{2,3},{3,4},{4,5},{5,6},{6,7},{7,8},{8,9},{9,10},{10,1... | collective-permute-start | bytes 552968 | tf_op jit(solution)/shard_map/ppermute | solution.py:526
  25.6 28.2 %all-to-all-start.1 = ((f32[32,1,640]{2,1,0:T(1,128)}), f32[32,1,640]{2,1,0:T(1,128)S(1)}, u32[]{:S(2)}, u32[]{:S(2)}) async-start(f32[32,1,640]{2,1,0:T(1,128)} %get-tuple-element.7), calls=%async_computation.1 | async-start | bytes 163840 | tf_op jit(solution)/shard_map/all_to_all | solution.py:563
  40.0 13.7 %copy-start = (f32[3,3]{1,0:T(4,128)S(1)}, f32[3,3]{1,0:T(4,128)}, u32[]{:S(2)}) copy-start(f32[3,3]{1,0:T(4,128)} %applied_ref.1) | copy-start | bytes 112
